TPU v7x, 256 devices: a whole 4x4x8 slice. The times are simulated.
256 devices in a mesh: ctx: 32 (over x, y, core), tp: 8 (over z).
Axes of the slice: x: 4, y: 4, z: 8, core: 2. Of those that a mesh axis runs over, the one named last changes fastest.
Arguments:
- queries: bfloat16 [4096, 128, 576], P('ctx', 'tp'), may hold values from -73 to 73
- latent_block_cache: bfloat16 [512, 128, 576], P('ctx'), may hold values from -12 to 12
- selected_block_lists: int32 [4096, 4], P('ctx'), may hold values from 0 to 511, as said below
- output_gradient: bfloat16 [4096, 7168], P(None, 'ctx'), may hold values from -6 to 6
- output_weight: bfloat16 [16384, 7168], P('tp', 'ctx'), may hold values from -0.046875 to 0.046875
- adapter_down: bfloat16 [32, 16384], P(None, 'tp'), may hold values from -0.046875 to 0.046875
- adapter_up: bfloat16 [32, 7168], P(None, 'ctx'), may hold values from -0.119628906 to 0.119628906
- value_up_map: bfloat16 [128, 512, 128], P('tp'), may hold values from -0.25 to 0.25
- saved_head_input: bfloat16 [4096, 16384], P('ctx', 'tp'), may hold values from -6 to 6
Outputs:
- query_grads: bfloat16 [4096, 128, 576], P('ctx', 'tp')
- cache_grads: float32 [512, 128, 576], P('ctx', 'tp')
- down_gradient: float32 [32, 16384], P(None, 'tp')
- up_gradient: float32 [32, 7168], P(None, 'ctx')
Inputs may be any that keep to these rules, and one draw needn't show every extreme that they name: `selected_block_lists`: each query names 4 different blocks. The queries of one ctx index fall into 2 equal groups of consecutive queries; each group names exactly 6 distinct blocks together, and different groups of one ctx index name different blocks, so that the ctx index names exactly 12. At most 1 of them lie among the 16 blocks held by one ctx index, and the last ctx index gives exactly 1 to every ctx index.
All inputs are finite; a program needn't handle non-finite values.
Results may differ from a plain program's by a relative error of at most 0.04.
Values may be sent and summed in bfloat16 or wider, within the bound.
No kernel may reach another device: no remote copies, remote signals or barrier semaphores. Data moves between devices by JAX's collectives and lax.ppermute only.
A program may use at most 192 MiB of HBM per device.

v0:
```python
import jax
import jax.numpy as jnp
from jax import lax
from jax.sharding import PartitionSpec as P

GCANDS = 6
QGROUPS = 2
CANDS = 12


SCORE_SCALE = 192.0 ** (-0.5)
ADAPTER_SCALE = 2.0


def collect_owned(returned, served_ids, blocks_dev):
    slot_count = served_ids.shape[0] * served_ids.shape[1]
    one_hot = (
        served_ids.reshape(slot_count)[:, None] == jnp.arange(blocks_dev, dtype=jnp.int32)[None, :]
    ).astype(jnp.float32)
    flat = returned.reshape(slot_count, returned.shape[2], returned.shape[3])
    return jnp.einsum("sb,srk->brk", one_hot, flat, precision=lax.Precision.HIGHEST)


def attend_group(query_part, grad_part, key_rows, picked, latent_width):
    query_count = query_part.shape[0]
    heads_dev = query_part.shape[1]
    width = query_part.shape[2]
    row_total = query_count * heads_dev
    query_flat = query_part.reshape(row_total, width)
    grad_flat = grad_part.reshape(row_total, latent_width)
    cand_count = picked.shape[1]
    block_rows = key_rows.shape[0] // cand_count
    scores = SCORE_SCALE * jnp.einsum(
        "nk,mk->nm", query_flat, key_rows, preferred_element_type=jnp.float32
    )
    selected = jnp.broadcast_to(
        picked[:, None, :, None], (query_count, heads_dev, cand_count, block_rows)
    )
    selected = selected.reshape(row_total, cand_count * block_rows)
    scores = jnp.where(selected, scores, -jnp.inf)
    highest = jnp.max(scores, axis=1, keepdims=True)
    weights = jnp.exp(scores - highest)
    weights = weights / jnp.sum(weights, axis=1, keepdims=True)
    weights_round = weights.astype(jnp.bfloat16)
    latent_keys = key_rows[:, :latent_width]
    prob_grads = jnp.einsum("nl,ml->nm", grad_flat, latent_keys, preferred_element_type=jnp.float32)
    row_delta = jnp.sum(weights * prob_grads, axis=1, keepdims=True)
    score_grads = (weights * (prob_grads - row_delta) * SCORE_SCALE).astype(jnp.bfloat16)
    query_out = jnp.dot(score_grads, key_rows, preferred_element_type=jnp.float32).astype(
        jnp.bfloat16
    )
    query_out = query_out.reshape(query_count, heads_dev, width)
    key_grads = jnp.einsum("nm,nk->mk", score_grads, query_flat, preferred_element_type=jnp.float32)
    latent_grads = key_grads[:, :latent_width] + jnp.einsum(
        "nm,nl->ml", weights_round, grad_flat, preferred_element_type=jnp.float32
    )
    key_grads = jnp.concatenate([latent_grads, key_grads[:, latent_width:]], axis=1)
    return (query_out, key_grads.reshape(cand_count, block_rows, width))


def shards(
    queries,
    latent_block_cache,
    selected_block_lists,
    output_gradient,
    output_weight,
    adapter_down,
    adapter_up,
    value_up_map,
    saved_head_input,
):
    ctx_size = lax.axis_size("ctx")
    capacity = max(1, 2 * CANDS // ctx_size)
    query_count = queries.shape[0]
    heads_dev = queries.shape[1]
    width = queries.shape[2]
    blocks_dev = latent_block_cache.shape[0]
    block_rows = latent_block_cache.shape[1]
    latent_width = value_up_map.shape[1]
    value_width = value_up_map.shape[2]
    all_blocks = blocks_dev * ctx_size
    listed = selected_block_lists.reshape(-1)
    present = jnp.any(listed[:, None] == jnp.arange(all_blocks, dtype=jnp.int32)[None, :], axis=0)
    owned = present.reshape(ctx_size, blocks_dev).astype(jnp.int32)
    ranking = jnp.cumsum(owned, axis=1)
    places = jnp.arange(1, capacity + 1, dtype=jnp.int32)
    matches = (owned[:, None, :] == 1) & (ranking[:, None, :] == places[None, :, None])
    wanted = jnp.sum(
        jnp.where(matches, jnp.arange(blocks_dev, dtype=jnp.int32)[None, None, :], 0), axis=2
    )
    usable = jnp.any(matches, axis=2)
    served_ids = lax.all_to_all(wanted, "ctx", split_axis=0, concat_axis=0, tiled=True)
    served = latent_block_cache[served_ids]
    fetched = lax.all_to_all(served, "ctx", split_axis=0, concat_axis=0, tiled=True)
    slot_count = ctx_size * capacity
    usable_flat = usable.reshape(slot_count).astype(jnp.int32)
    slot_rank = jnp.cumsum(usable_flat)
    chosen_slot = (usable_flat[None, :] == 1) & (
        slot_rank[None, :] == jnp.arange(1, CANDS + 1, dtype=jnp.int32)[:, None]
    )
    cand_slot = jnp.sum(
        jnp.where(chosen_slot, jnp.arange(slot_count, dtype=jnp.int32)[None, :], 0), axis=1
    )
    slot_block = (jnp.arange(ctx_size, dtype=jnp.int32)[:, None] * blocks_dev + wanted).reshape(
        slot_count
    )
    cand_block = slot_block[cand_slot]
    cand_rows = fetched.reshape(slot_count, block_rows, width)[cand_slot]
    adapter_low = jnp.einsum(
        "iz,nz->in", output_gradient, adapter_up, preferred_element_type=jnp.float32
    )
    down_single_float = adapter_down.astype(jnp.float32)
    direct_result = jnp.einsum(
        "qd,hd->qh", output_gradient, output_weight, preferred_element_type=jnp.float32
    )
    direct_result = direct_result + ADAPTER_SCALE * jnp.dot(
        adapter_low, down_single_float, precision=lax.Precision.HIGHEST
    )
    summed_result = lax.psum_scatter(
        jnp.concatenate([direct_result, adapter_low], axis=1).astype(jnp.bfloat16),
        "ctx",
        scatter_dimension=0,
        tiled=True,
    ).astype(jnp.float32)
    head_feature_width = output_weight.shape[0]
    head_grads = summed_result[:, :head_feature_width].astype(jnp.bfloat16)
    adapter_gradient = (ADAPTER_SCALE * summed_result[:, head_feature_width:]).astype(jnp.bfloat16)
    row_portion = jnp.einsum(
        "ng,eg->ne", saved_head_input, adapter_down, preferred_element_type=jnp.float32
    )
    row_total_part = lax.psum(row_portion, "tp")
    gathered_rows = lax.all_gather(row_total_part, "ctx", axis=0, tiled=True)
    adapter_rows = gathered_rows.astype(jnp.bfloat16)
    up_gradient = ADAPTER_SCALE * jnp.einsum(
        "jn,jh->nh", adapter_rows, output_gradient, preferred_element_type=jnp.float32
    )
    down_piece_part = jnp.einsum(
        "gm,gi->mi", adapter_gradient, saved_head_input, preferred_element_type=jnp.float32
    )
    down_gradient = lax.psum(down_piece_part.astype(jnp.bfloat16), "ctx").astype(jnp.float32)
    out_grads = jnp.einsum(
        "qhv,hlv->qhl",
        head_grads.reshape(query_count, heads_dev, value_width),
        value_up_map,
        preferred_element_type=jnp.float32,
    ).astype(jnp.bfloat16)
    group_queries = query_count // QGROUPS
    query_parts = []
    cand_grads = jnp.zeros((CANDS, block_rows, width), jnp.float32)
    for group_number in range(QGROUPS):
        first_query = group_number * group_queries
        lists_part = selected_block_lists[first_query : first_query + group_queries]
        touched = jnp.any(lists_part.reshape(-1)[:, None] == cand_block[None, :], axis=0).astype(
            jnp.int32
        )
        touch_rank = jnp.cumsum(touched)
        touch_hits = (touched[None, :] == 1) & (
            touch_rank[None, :] == jnp.arange(1, GCANDS + 1, dtype=jnp.int32)[:, None]
        )
        group_slots = jnp.sum(
            jnp.where(touch_hits, jnp.arange(CANDS, dtype=jnp.int32)[None, :], 0), axis=1
        )
        key_rows = cand_rows[group_slots].reshape(GCANDS * block_rows, width)
        picked = jnp.any(lists_part[:, :, None] == cand_block[group_slots][None, None, :], axis=1)
        query_out, group_grads = attend_group(
            queries[first_query : first_query + group_queries],
            out_grads[first_query : first_query + group_queries],
            key_rows,
            picked,
            latent_width,
        )
        query_parts.append(query_out)
        cand_grads = cand_grads.at[group_slots].add(group_grads)
    query_grads = jnp.concatenate(query_parts, axis=0)
    slot_grads = jnp.zeros((slot_count, block_rows, width), jnp.float32)
    slot_grads = slot_grads.at[cand_slot].set(cand_grads)
    slot_grads = slot_grads.reshape(ctx_size, capacity, block_rows, width)
    returned = lax.all_to_all(
        slot_grads.astype(jnp.bfloat16), "ctx", split_axis=0, concat_axis=0, tiled=True
    ).astype(slot_grads.dtype)
    owned_grads = collect_owned(returned, served_ids, blocks_dev)
    cache_grads = lax.psum_scatter(
        owned_grads.astype(jnp.bfloat16), "tp", scatter_dimension=1, tiled=True
    ).astype(jnp.float32)
    return (query_grads, cache_grads, down_gradient, up_gradient)


def solution(mesh):
    placed = (
        P("ctx", "tp", None),
        P("ctx", None, None),
        P("ctx", None),
        P(None, "ctx"),
        P("tp", "ctx"),
        P(None, "tp"),
        P(None, "ctx"),
        P("tp", None, None),
        P("ctx", "tp"),
    )
    return jax.shard_map(
        shards,
        mesh=mesh,
        in_specs=placed,
        out_specs=(P("ctx", "tp", None), P("ctx", "tp", None), P(None, "tp"), P(None, "ctx")),
        check_vma=False,
    )
```

profile of v0, /device:TPU:2, one launch (start us, length us, event | category | flops | bytes accessed | tf_op | source)
XLA Modules:
  0.0 490.9 jit_solution(1274963948583186451)
XLA Ops:
  7.2 2.1 fusion.41
  9.4 18.1 %fusion.44 = f32[4096,2048]{0,1:T(8,128)} fusion(f32[4096,32]{0,1:T(8,128)S(1)} %get-tuple-element.47, bf16[32,2048]{1,0:T(8,128)(2,1)} %param.14), kind=kOutput, calls=%fused_computation.98 | convolution fusion | flops 3221225472 | bytes 34209792 | tf_op jit(solution)/shard_map/dot_general | solution.py:116
  27.5 16.9 %add_convert_fusion = bf16[4096,2048]{0,1:T(8,128)(2,1)} fusion(f32[4096,2048]{0,1:T(8,128)} %fusion.44, bf16[4096,224]{0,1:T(8,128)(2,1)S(1)} %copy-done.2, bf16[2048,224]{0,1:T(8,128)(2,1)S(1)} %copy-done.19), kind=kOutput, calls=%fused_computation.10 | convolution fusion | flops 3783262208 | bytes 53084160 | tf_op jit(solution)/shard_map/qd,hd->qh/dot_general | solution.py:113
  44.4 14.1 %pad_maximum_fusion = bf16[4096,2080]{0,1:T(8,128)(2,1)} fusion(bf16[4096,32]{0,1:T(8,128)(2,1)S(1)} %get-tuple-element.46, bf16[4096,2048]{0,1:T(8,128)(2,1)} %add_convert_fusion), kind=kLoop, calls=%fused_computation.11 | loop fusion | flops 34078720 | bytes 34078720 | tf_op jit(solution)/shard_map/concatenate | solution.py:120
  58.4 21.9 %copy.128 = bf16[4096,2080]{1,0:T(8,128)(2,1)} copy(bf16[4096,2080]{0,1:T(8,128)(2,1)} %pad_maximum_fusion) | data formatting | bytes 34078720
  82.2 13.6 %all_to_all.19 = s32[32,1,1]{2,1,0:T(1,128)S(1)} all-to-all(s32[32,1,1]{2,1,0:T(1,128)S(1)} %copy.104), channel_id=1, replica_groups=mesh['ctx'=32,'tp'=8] {'ctx'}, dimensions={0} | all-to-all | bytes 256 | tf_op jit(solution)/shard_map/all_to_all | solution.py:92
  95.8 1.2 fusion.35
  97.0 3.3 gather_fusion.2
  100.4 6.3 %all-to-all-start.1 = ((bf16[32,1,128,576]{2,3,1,0:T(8,128)(2,1)}), bf16[32,1,128,576]{2,3,1,0:T(8,128)(2,1)}, u32[]{:S(2)}, u32[]{:S(2)}) async-start(bf16[32,1,128,576]{2,3,1,0:T(8,128)(2,1)} %bitcast.95), calls=%async_computation.1 | async-start | bytes 9437184 | tf_op jit(solution)/shard_map/all_to_all | solution.py:94
  111.4 1.8 copy.115
  113.2 5.1 %fusion.37 = (bf16[64,16,576]{0,2,1:T(8,128)(2,1)S(1)}, bf16[64,16,576]{0,2,1:T(8,128)(2,1)}) fusion(bf16[128,16,576]{0,2,1:T(8,128)(2,1)} %param.9), kind=kLoop, calls=%fused_computation.91 | loop fusion | bytes 4718592 | tf_op jit(solution)/shard_map/slice | solution.py:166
  118.3 4.7 copy.114
  123.9 1.8 copy.107
  125.6 3.4 copy.106
  129.0 50.9 %all-to-all-done.1 = bf16[32,1,128,576]{2,3,1,0:T(8,128)(2,1)} async-done(((bf16[32,1,128,576]{2,3,1,0:T(8,128)(2,1)}), bf16[32,1,128,576]{2,3,1,0:T(8,128)(2,1)}, u32[]{:S(2)}, u32[]{:S(2)}) %all-to-all-start.1) | async-done | bytes 4718624 | tf_op jit(solution)/shard_map/all_to_all | solution.py:94
  179.9 3.5 gather_fusion.3
  184.2 1.6 gather_fusion.4
  185.8 1.3 copy.113
  187.1 1.9 copy.105
  189.1 3.3 fusion.42
  192.9 1.8 copy-done.14
  195.0 1.5 fusion.43
  196.6 1.7 copy-done.6
  198.7 30.0 %reduce-scatter.7.cloned.1.call-done = bf16[128,2080]{1,0:T(8,128)(2,1)} async-done(((bf16[4096,2080]{1,0:T(8,128)(2,1)}), bf16[128,2080]{1,0:T(8,128)(2,1)}) %reduce-scatter.7.cloned.1.call-update) | async-done | bytes 532496
  228.7 1.1 slice.75
  230.1 2.4 convert_bitcast_fusion.1
  233.3 1.1 copy-done.7
  234.6 1.1 multiply_reduce_fusion.1
  235.7 0.9 multiply_convert_fusion.1
  237.0 1.1 fusion.45
  238.2 1.1 slice_add_fusion.1
  239.9 0.8 copy-done.5
  240.9 1.1 multiply_reduce_fusion
  242.0 0.9 multiply_convert_fusion
  243.4 1.3 fusion.46
  244.7 2.3 slice_add_fusion
  247.1 1.8 copy.118
  248.9 1.9 copy.119
  250.7 2.8 pad_maximum_fusion.3
  253.5 2.8 copy.120
  256.3 2.8 copy.121
  259.1 2.2 broadcast_in_dim.66
  261.3 4.2 scatter_fusion
  265.5 4.8 scatter_fusion.1
  270.3 4.8 broadcast_in_dim.65
  275.0 7.8 %scatter_fusion.2 = f32[32,128,576]{1,2,0:T(8,128)} fusion(f32[32,128,576]{1,2,0:T(8,128)} %broadcast_in_dim.65, s32[12]{0:T(128)S(1)} %fusion.29, f32[12,128,576]{1,2,0:T(8,128)} %scatter_fusion.1), kind=kCustom, calls=%fused_computation.9 | custom fusion | bytes 10616880 | tf_op jit(solution)/shard_map/scatter | solution.py:176
  282.8 6.6 %convert_bitcast_fusion = bf16[32,1,128,576]{2,3,1,0:T(8,128)(2,1)} fusion(f32[32,128,576]{1,2,0:T(8,128)} %scatter_fusion.2), kind=kLoop, calls=%fused_computation.15 | loop fusion | flops 2359296 | bytes 14155776 | tf_op jit(solution)/shard_map/convert_element_type | solution.py:179
  289.4 5.8 %all-to-all-start.2 = ((bf16[32,1,128,576]{2,3,1,0:T(8,128)(2,1)}), bf16[32,1,128,576]{2,3,1,0:T(8,128)(2,1)}, u32[]{:S(2)}, u32[]{:S(2)}) async-start(bf16[32,1,128,576]{2,3,1,0:T(8,128)(2,1)} %convert_bitcast_fusion), calls=%async_computation.2 | async-start | bytes 9437184 | tf_op jit(solution)/shard_map/all_to_all | solution.py:178
  295.3 0.9 convolution_convert_fusion
  296.3 56.1 %all-to-all-done.2 = bf16[32,1,128,576]{2,3,1,0:T(8,128)(2,1)} async-done(((bf16[32,1,128,576]{2,3,1,0:T(8,128)(2,1)}), bf16[32,1,128,576]{2,3,1,0:T(8,128)(2,1)}, u32[]{:S(2)}, u32[]{:S(2)}) %all-to-all-start.2) | async-done | bytes 4718624 | tf_op jit(solution)/shard_map/all_to_all | solution.py:178
  352.4 6.6 %fusion.7 = bf16[16,128,576]{1,0,2:T(8,128)(2,1)} fusion(bf16[32,1,128,576]{2,3,1,0:T(8,128)(2,1)} %all-to-all-done.2, s32[32]{0:T(128)S(1)} %get-tuple-element.24), kind=kOutput, calls=%fused_computation.33 | convolution fusion | flops 76677632 | bytes 7078016 | tf_op jit(solution)/shard_map/sb,srk->brk/dot_general | solution.py:21
  359.0 5.5 %copy.124 = bf16[16,128,576]{2,0,1:T(8,128)(2,1)} copy(bf16[16,128,576]{1,0,2:T(8,128)(2,1)} %fusion.7) | data formatting | bytes 4718592 | tf_op jit(solution)/shard_map/convert_element_type | solution.py:183
  364.8 30.2 %psum.15 = bf16[128,32]{0,1:T(8,128)(2,1)S(1)} all-reduce(f32[128,32]{0,1:T(8,128)S(1)} %fusion.47), channel_id=1, replica_groups=mesh['ctx'=32,'tp'=8] {'tp'}, use_global_device_ids=true, to_apply=%region_26.27 | all-reduce | flops 4096 | bytes 24576 | tf_op jit(solution)/shard_map/psum | solution.py:131
  395.1 26.1 %all_gather.3 = bf16[4096,32]{0,1:T(8,128)(2,1)S(1)} all-gather(bf16[128,32]{0,1:T(8,128)(2,1)S(1)} %psum.15), channel_id=1, replica_groups=mesh['ctx'=32,'tp'=8] {'ctx'}, dimensions={0}, use_global_device_ids=true | all-gather | bytes 270336 | tf_op jit(solution)/shard_map/all_gather | solution.py:132
  421.2 1.3 convolution_multiply_fusion
  422.5 2.9 convolution_convert_fusion.1
  425.4 1.4 copy.117
  426.9 2.3 convolution_convert_fusion.2
  429.2 1.4 copy.110
  430.6 3.7 pad_maximum_fusion.1
  434.4 4.7 copy.125
  439.0 1.6 convert_element_type.163
  440.7 41.6 %reduce-scatter.5.cloned.1.call-done = bf16[16,16,576]{2,0,1:T(8,128)(2,1)} async-done(((bf16[16,128,576]{2,0,1:T(8,128)(2,1)}), bf16[16,16,576]{2,0,1:T(8,128)(2,1)}) %reduce-scatter.5.cloned.1.call-update) | async-done | bytes 294928 | tf_op jit(solution)/shard_map/reduce_scatter | solution.py:182
  482.2 1.9 copy.126
  (115 shorter events, 13.1 us)
Async XLA Ops:
  7.2 89.8 %copy-start = (bf16[16,128,576]{1,2,0:T(8,128)(2,1)S(1)}, bf16[16,128,576]{1,2,0:T(8,128)(2,1)}, u32[]{:S(2)}) copy-start(bf16[16,128,576]{1,2,0:T(8,128)(2,1)} %param.10) | copy-start | bytes 7077892
  7.2 221.5 %reduce-scatter.7.cloned.1.call-start = ((), (), s32[]{:S(2)}) async-start(), calls=%async_computation.7 | async-start | bytes 18382848
  9.3 18.1 %copy-start.2 = (bf16[4096,224]{0,1:T(8,128)(2,1)S(1)}, bf16[4096,224]{0,1:T(8,128)(2,1)}, u32[]{:S(2)}) copy-start(bf16[4096,224]{0,1:T(8,128)(2,1)} %param.12) | copy-start | bytes 5505028
  9.3 18.1 %copy-start.19 = (bf16[2048,224]{0,1:T(8,128)(2,1)S(1)}, bf16[2048,224]{0,1:T(8,128)(2,1)}, u32[]{:S(2)}) copy-start(bf16[2048,224]{0,1:T(8,128)(2,1)} %param.13) | copy-start | bytes 2752516
  80.3 0.7 copy-start.24
  100.4 79.6 %all-to-all-start.1 = ((bf16[32,1,128,576]{2,3,1,0:T(8,128)(2,1)}), bf16[32,1,128,576]{2,3,1,0:T(8,128)(2,1)}, u32[]{:S(2)}, u32[]{:S(2)}) async-start(bf16[32,1,128,576]{2,3,1,0:T(8,128)(2,1)} %bitcast.95), calls=%async_computation.1 | async-start | bytes 9437184 | tf_op jit(solution)/shard_map/all_to_all | solution.py:94
  185.8 3.3 copy-start.12
  189.0 3.8 copy-start.16
  192.4 4.2 copy-start.4
  192.4 2.3 copy-start.14
  192.4 2.7 copy-start.22
  196.6 1.7 copy-start.6
  232.4 1.9 copy-start.7
  232.5 2.1 copy-start.17
  235.7 1.3 copy-start.15
  237.0 2.3 copy-start.9
  238.1 1.2 copy-start.20
  238.1 2.5 copy-start.5
  238.2 2.8 copy-start.18
  242.0 1.3 copy-start.13
  243.4 1.3 copy-start.11
  244.7 2.3 copy-start.21
  244.7 2.3 slice-start
  247.1 3.6 slice-start.1
  289.4 5.9 %slice-start.2 = ((bf16[128,2080]{1,0:T(8,128)(2,1)}), bf16[128,32]{1,0:T(8,128)(2,1)S(1)}, s32[]{:S(2)}) async-start(bf16[128,2080]{1,0:T(8,128)(2,1)} %reduce-scatter.7.cloned.1.call-done), calls=%async_computation.10 | async-start | bytes 65536 | tf_op jit(solution)/shard_map/slice | solution.py:127
  289.4 5.9 %copy-start.8 = (bf16[128,2048]{1,0:T(8,128)(2,1)S(1)}, bf16[128,2048]{1,0:T(8,128)(2,1)}, u32[]{:S(2)}) copy-start(bf16[128,2048]{1,0:T(8,128)(2,1)} %param.17) | copy-start | bytes 1572868
  289.4 63.0 %all-to-all-start.2 = ((bf16[32,1,128,576]{2,3,1,0:T(8,128)(2,1)}), bf16[32,1,128,576]{2,3,1,0:T(8,128)(2,1)}, u32[]{:S(2)}, u32[]{:S(2)}) async-start(bf16[32,1,128,576]{2,3,1,0:T(8,128)(2,1)} %convert_bitcast_fusion), calls=%async_computation.2 | async-start | bytes 9437184 | tf_op jit(solution)/shard_map/all_to_all | solution.py:178
  295.2 143.8 %all-reduce.2.cloned.1.call-start = ((), (), s32[]{:S(2)}) async-start(), calls=%async_computation.6 | async-start | bytes 262144 | tf_op jit(solution)/shard_map/psum | solution.py:140
  296.3 186.0 %reduce-scatter.5.cloned.1.call-start = ((), (), s32[]{:S(2)}) async-start(), calls=%async_computation.5 | async-start | bytes 2949120 | tf_op jit(solution)/shard_map/reduce_scatter | solution.py:182
  359.0 5.5 %copy-start.23 = (bf16[32,2048]{1,0:T(8,128)(2,1)S(1)}, bf16[32,2048]{1,0:T(8,128)(2,1)}, u32[]{:S(2)}) copy-start(bf16[32,2048]{1,0:T(8,128)(2,1)} %param.14) | copy-start | bytes 393220
  359.0 62.2 %copy-start.3 = (bf16[4096,224]{0,1:T(8,128)(2,1)S(1)}, bf16[4096,224]{0,1:T(8,128)(2,1)}, u32[]{:S(2)}) copy-start(bf16[4096,224]{0,1:T(8,128)(2,1)} %param.12) | copy-start | bytes 5505028
  422.5 4.4 copy-start.10
  430.6 53.5 %copy-start.1 = (bf16[16,128,576]{1,2,0:T(8,128)(2,1)S(1)}, bf16[16,128,576]{1,2,0:T(8,128)(2,1)}, u32[]{:S(2)}) copy-start(bf16[16,128,576]{1,2,0:T(8,128)(2,1)} %param.10) | copy-start | bytes 7077892
Sparse Core Ops, SparseCore 0:
  80.5 148.1 reduce-scatter.6
  300.2 135.0 all-reduce.1
  437.8 44.3 reduce-scatter.4
where the time goes:
time: 499 us; the launch traced here: 491 us
  waiting for transfers between devices  179 us (36%)
  local copies, waits for them, and re-layouts  105 us (21%)
  blocking collectives  70 us (14%)
  matrix products  66.5 us (13%)
  other arithmetic  43.8 us (9%)
  between operations  14.5 us (3%)
  starting transfers between devices  12.2 us (2%)
    all_to_all x1, waiting for transfers between devices, shards(): lax.all_to_all(slot_grads.astype(jnp.bfloat16), 'ctx', split_axis=0, conc...  56.1 us
    all_to_all x1, waiting for transfers between devices, shards(): lax.all_to_all(served, 'ctx', split_axis=0, concat_axis=0, tiled=True)  50.9 us
    reduce_scatter x1, waiting for transfers between devices, shards(): lax.psum_scatter(owned_grads.astype(jnp.bfloat16), 'tp', scatter_dimensio...  41.6 us
    unnamed x58, local copies, waits for them, and re-layouts  37.5 us
    psum x1, blocking collectives, shards(): row_total_part = lax.psum(row_portion, 'tp')  30.2 us
    unnamed x4, waiting for transfers between devices  30.1 us
    all_gather x1, blocking collectives, shards(): gathered_rows = lax.all_gather(row_total_part, 'ctx', axis=0, tiled=True)  26.1 us
    dot_general x1, matrix products, shards(): jnp.dot(adapter_low, down_single_float, precision=lax.Precision.HIGHEST)  18.1 us
  transfers between devices with their start and end apart: 5, of which 4 were waited for; matrix products, arithmetic and copies ran while one was open for 15% of the time, Pallas kernels for 0%

commit v1 on v0

v1 whole, which is shorter than its diff:
```python
import functools

import jax
import jax.numpy as jnp
from jax import lax
from jax.experimental import pallas as pl
from jax.experimental.pallas import tpu as pltpu
from jax.sharding import Mesh, PartitionSpec as P

SCORE_SCALE = 192.0 ** (-0.5)
ADAPTER_SCALE = 2.0

NX = 4
NY = 4
NCORE = 2
NCTX = 32
NTP = 8
GROUPS = 2
GSLOTS = 6
SLOTS = 12
BLOCK = 128
WIDTH = 576
LATENT = 512
VALUE = 128
HEADS_DEV = 16
QRY_DEV = 128
GQ = 64
RANK = 32
FEATS = 224
HEAD_IN = 2048
PIECE = BLOCK // NTP
SLOT_LANES = 896
GROUP_ROWS = GSLOTS * BLOCK
MASKED = -1e30

bf16 = jnp.bfloat16
f32 = jnp.float32

NN = (((1,), (0,)), ((), ()))
NT = (((1,), (1,)), ((), ()))
TN = (((0,), (0,)), ((), ()))


def mm(a, b, dims):
    return lax.dot_general(a, b, dims, preferred_element_type=f32)


def params(mib):
    return pltpu.CompilerParams(vmem_limit_bytes=mib * 1024 * 1024)


def cost(flops, nbytes):
    return pl.CostEstimate(flops=int(flops), bytes_accessed=int(nbytes), transcendentals=0)


def smem():
    return pl.BlockSpec(memory_space=pltpu.SMEM)


def vmem():
    return pl.BlockSpec(memory_space=pltpu.VMEM)


def prep_kernel(place, g_ref, up_ref, w_ref, down_ref, mine, other, low_out, wcat, turned):
    step = pl.program_id(0)
    core = place[2]
    tp = place[3]

    @pl.when(step == 0)
    def _():
        wcat[:FEATS, :] = w_ref[...]
        wcat[FEATS:, :] = (ADAPTER_SCALE * down_ref[...].astype(f32)).astype(bf16)

    g = g_ref[...]
    low = mm(up_ref[...], g, NN).astype(bf16)
    turned[...] = jnp.concatenate([g, low], axis=0).T
    mine[0] = turned[pl.ds(pl.multiple_of(core * QRY_DEV, QRY_DEV), QRY_DEV), :]
    other[0] = turned[pl.ds(pl.multiple_of((1 - core) * QRY_DEV, QRY_DEV), QRY_DEV), :]
    for half in range(2):
        start = pl.multiple_of(half * QRY_DEV + tp * PIECE, PIECE)
        low_out[half] = turned[pl.ds(start, PIECE), 128:]


def prep(place, g_t, up, w_t, down):
    pairs = NX * NY
    return pl.pallas_call(
        prep_kernel,
        grid_spec=pltpu.PrefetchScalarGridSpec(
            num_scalar_prefetch=1,
            grid=(pairs,),
            in_specs=[
                pl.BlockSpec((FEATS, 2 * QRY_DEV), lambda s, p: (0, s)),
                pl.BlockSpec((RANK, FEATS), lambda s, p: (0, 0)),
                pl.BlockSpec((FEATS, HEAD_IN), lambda s, p: (0, 0)),
                pl.BlockSpec((RANK, HEAD_IN), lambda s, p: (0, 0)),
            ],
            out_specs=[
                pl.BlockSpec((1, QRY_DEV, 256), lambda s, p: (s, 0, 0)),
                pl.BlockSpec((1, QRY_DEV, 256), lambda s, p: (s, 0, 0)),
                pl.BlockSpec((2, PIECE, 128), lambda s, p: (s, 0, 0)),
                pl.BlockSpec((256, HEAD_IN), lambda s, p: (0, 0)),
            ],
            scratch_shapes=[pltpu.VMEM((256, 256), bf16)],
        ),
        out_shape=[
            jax.ShapeDtypeStruct((pairs, QRY_DEV, 256), bf16),
            jax.ShapeDtypeStruct((pairs, QRY_DEV, 256), bf16),
            jax.ShapeDtypeStruct((NCTX, PIECE, 128), bf16),
            jax.ShapeDtypeStruct((256, HEAD_IN), bf16),
        ],
        compiler_params=params(24),
        cost_estimate=cost(1e8, 6e6),
    )(place, g_t, up, w_t, down)


def head_kernel(place, m0, m1, p0, p1, w_own, w_pair, *outs):
    (a_own, a_p1, a_m1, a_p2, a_m2, b_own, b_p1, b_m1, b_p2, b_m2) = outs
    step = pl.program_id(0)
    own = jnp.concatenate([m0[0], m1[0]], axis=0)
    pair = jnp.concatenate([p0[0], p1[0]], axis=0)
    half = HEAD_IN // 2
    for part in range(2):
        cols = slice(part * half, (part + 1) * half)
        both = mm(own, w_own[:, cols], NN) + mm(pair, w_pair[:, cols], NN)
        both = both.astype(bf16)
        group_a = [both[0:GQ], both[2 * GQ : 3 * GQ]]
        group_b = [both[GQ : 2 * GQ], both[3 * GQ : 4 * GQ]]
        a_steps = {0: a_own, 1: a_own, 2: a_p2, 3: a_p1, 4: a_p1, 5: a_m1, 6: a_m1, 7: a_m2}
        for number, ref in a_steps.items():

            @pl.when(step == number)
            def _(ref=ref):
                ref[0, :, cols] = group_a[0]
                ref[1, :, cols] = group_a[1]

        b_steps = [
            (b_own, b_p2),
            (b_p1, b_m1),
            (b_own, b_p2),
            (b_p1, b_m1),
            (b_own, b_p1),
            (b_m1, b_m2),
            (b_own, b_p1),
            (b_m1, b_m2),
        ]
        for number, refs in enumerate(b_steps):

            @pl.when(step == number)
            def _(refs=refs):
                refs[0][0, :, cols] = group_b[0]
                refs[1][0, :, cols] = group_b[1]


def head_partials(place, mine, theirs, w_own, w_pair):
    def row(number):
        def index(s, p):
            x = lax.rem(p[0] + s // 2, NX)
            y = lax.rem(p[1] + 2 * lax.rem(s, 2) + number, NY)
            return (x * NY + y, 0, 0)

        return pl.BlockSpec((1, QRY_DEV, 256), index)

    def whole():
        return pl.BlockSpec((256, HEAD_IN), lambda s, p: (0, 0))

    def past(s, *bounds):
        total = 0
        for b in bounds:
            total = total + (s > b).astype(jnp.int32)
        return total

    def out(count, block, index):
        return (
            pl.BlockSpec((block, GQ, HEAD_IN), lambda s, p: (index(s), 0, 0)),
            jax.ShapeDtypeStruct((count, GQ, HEAD_IN), bf16),
        )

    outs = [
        out(4, 2, lambda s: past(s, 0)),
        out(4, 2, lambda s: past(s, 3)),
        out(4, 2, lambda s: past(s, 5)),
        out(2, 2, lambda s: 0),
        out(2, 2, lambda s: 0),
        out(4, 1, lambda s: past(s, 1, 3, 5)),
        out(4, 1, lambda s: past(s, 1, 3, 4)),
        out(4, 1, lambda s: past(s, 1, 3, 5)),
        out(2, 1, lambda s: past(s, 0)),
        out(2, 1, lambda s: past(s, 5)),
    ]
    return pl.pallas_call(
        head_kernel,
        grid_spec=pltpu.PrefetchScalarGridSpec(
            num_scalar_prefetch=1,
            grid=(8,),
            in_specs=[row(0), row(1), row(0), row(1), whole(), whole()],
            out_specs=[o[0] for o in outs],
        ),
        out_shape=[o[1] for o in outs],
        compiler_params=params(32),
        cost_estimate=cost(4.3e9, 13e6),
    )(place, mine, mine, theirs, theirs, w_own, w_pair)


def shift(value, axis, size, by):
    return lax.ppermute(value, axis, [(i, (i + by) % size) for i in range(size)])


def add(*terms):
    total = terms[0].astype(f32)
    for t in terms[1:]:
        total = total + t.astype(f32)
    return total.astype(bf16)


def ring_first(axis, own, plus1, minus1, plus2, minus2):
    from_minus = shift(plus1, axis, 4, 1)
    from_plus = shift(minus1, axis, 4, -1)
    return from_minus, from_plus


def reduce_second(axis, total):
    h = GQ // 2
    p1 = jnp.concatenate([total[2][:h], total[1][h:]], axis=0)
    m1 = jnp.concatenate([total[2][h:], total[3][:h]], axis=0)
    from_minus = shift(p1, axis, 4, 1)
    from_plus = shift(m1, axis, 4, -1)
    p2 = add(total[1][:h], from_minus[:h])
    m2 = add(total[3][h:], from_plus[:h])
    last_minus = shift(p2, axis, 4, 1)
    last_plus = shift(m2, axis, 4, -1)
    top = add(total[0][:h], from_plus[h:], last_minus)
    low = add(total[0][h:], from_minus[h:], last_plus)
    return jnp.concatenate([top, low], axis=0)


def turn_kernel(place, cache_ref, out_ref, turned):
    start = pl.multiple_of(place[3] * PIECE, PIECE)
    for b in range(cache_ref.shape[0]):
        turned[...] = cache_ref[b].T
        out_ref[b] = turned[pl.ds(start, PIECE), :]


def turn_cache(place, cache_t):
    blocks = cache_t.shape[0]
    return pl.pallas_call(
        turn_kernel,
        in_specs=[smem(), vmem()],
        out_specs=vmem(),
        out_shape=jax.ShapeDtypeStruct((blocks, PIECE, WIDTH), bf16),
        scratch_shapes=[pltpu.VMEM((BLOCK, WIDTH), bf16)],
        compiler_params=params(16),
        cost_estimate=cost(1e6, 3e6),
    )(place, cache_t)


def rows_kernel(saved_ref, down_ref, out_ref):
    rows_t = mm(down_ref[...], saved_ref[...], NT).astype(bf16)
    out_ref[:, :128] = rows_t[:16]
    out_ref[:, 128:] = rows_t[16:]


def adapter_rows(saved, down):
    return pl.pallas_call(
        rows_kernel,
        in_specs=[vmem(), vmem()],
        out_specs=vmem(),
        out_shape=jax.ShapeDtypeStruct((16, 256), bf16),
        compiler_params=params(8),
        cost_estimate=cost(1.7e7, 7e5),
    )(saved, down)


def serve_kernel(ids, cache_ref, low_ref, rows_ref, out_ref):
    lane = lax.broadcasted_iota(jnp.int32, (PIECE, 128), 1)
    rows = rows_ref[...]
    for s in range(NCTX):
        block = cache_ref[ids[s]]
        out_ref[s, :, :512] = block[:, :512]
        out_ref[s, :, 512:640] = low_ref[s]
        out_ref[s, :, 512:576] = block[:, 512:]
        out_ref[s, :, 640:] = rows


def serve(ids, cache_piece, low, rows):
    return pl.pallas_call(
        serve_kernel,
        in_specs=[smem(), vmem(), vmem(), vmem()],
        out_specs=vmem(),
        out_shape=jax.ShapeDtypeStruct((NCTX, PIECE, SLOT_LANES), bf16),
        compiler_params=params(8),
        cost_estimate=cost(1e6, 2e6),
    )(ids, cache_piece, low, rows)


def pick_kernel(chosen, got_ref, g_ref, out_ref, rows_all):
    for k in range(SLOTS):
        out_ref[k * PIECE : (k + 1) * PIECE, :] = got_ref[chosen[k], :, :WIDTH]
    low = got_ref[0, :, 512:640].astype(f32)
    for s in range(1, NCTX):
        low = low + got_ref[s, :, 512:640].astype(f32)
    for s in range(NCTX):
        rows_all[0:16, s * 128 : (s + 1) * 128] = got_ref[s, :, 640:768]
        rows_all[16:32, s * 128 : (s + 1) * 128] = got_ref[s, :, 768:896]
    up = mm(rows_all[...], g_ref[...], NT).astype(bf16)
    base = SLOTS * PIECE
    out_ref[base : base + 16, :] = jnp.zeros((16, WIDTH), bf16)
    out_ref[base : base + 16, 384:512] = low.astype(bf16)
    out_ref[base : base + 16, :FEATS] = up[:16]
    out_ref[base : base + 16, 256 : 256 + FEATS] = up[16:]


def pick(chosen, got, g_t):
    return pl.pallas_call(
        pick_kernel,
        in_specs=[smem(), vmem(), vmem()],
        out_specs=vmem(),
        out_shape=jax.ShapeDtypeStruct((SLOTS * PIECE + 16, WIDTH), bf16),
        scratch_shapes=[pltpu.VMEM((RANK, NCTX * QRY_DEV), bf16)],
        compiler_params=params(16),
        cost_estimate=cost(6e7, 3e6),
    )(chosen, got, g_t)


def gather_tp(own):
    pieces = [None] * NTP
    pieces[0] = own
    forward = own
    back = own
    for step in range(1, 5):
        forward = shift(forward, "tp", NTP, -1)
        pieces[step] = forward
        if step < 4:
            back = shift(back, "tp", NTP, 1)
            pieces[NTP - step] = back
    return pieces


def adapter_kernel(place, *refs):
    pieces = refs[:NTP]
    saved_ref, down_out, up_out, low = refs[NTP:]
    base = SLOTS * PIECE
    total = jnp.zeros((16, 512), f32)
    for d in range(NTP):
        rows = pieces[d][base : base + 16, :512]
        total = total + rows.astype(f32)
        where = lax.rem(place[3] + d, NTP)
        low[pl.ds(pl.multiple_of(where * PIECE, PIECE), PIECE), :] = rows[:, 384:]
    up_out[:16, :] = ADAPTER_SCALE * total[:, :FEATS]
    up_out[16:, :] = ADAPTER_SCALE * total[:, 256 : 256 + FEATS]
    grads = mm(low[...], saved_ref[...], TN)
    down_out[...] = (ADAPTER_SCALE * grads[96:, :]).astype(bf16)


def adapter_grads(place, pieces, saved):
    return pl.pallas_call(
        adapter_kernel,
        in_specs=[smem()] + [vmem()] * (NTP + 1),
        out_specs=[vmem(), vmem()],
        out_shape=[
            jax.ShapeDtypeStruct((RANK, HEAD_IN), bf16),
            jax.ShapeDtypeStruct((RANK, FEATS), f32),
        ],
        scratch_shapes=[pltpu.VMEM((QRY_DEV, 128), bf16)],
        compiler_params=params(16),
        cost_estimate=cost(7e7, 3e6),
    )(place, *pieces, saved)


def attend_kernel(*refs):
    pieces = refs[:NTP]
    q_ref, hg_a, hg_b, vu_ref, bias_ref, dq_ref = refs[NTP : NTP + 6]
    outs = refs[NTP + 6 : NTP + 15]
    keys, keys_t, acc, spread = refs[NTP + 15 :]
    step = pl.program_id(0)
    span = GSLOTS * PIECE

    @pl.when(step == 0)
    def _():
        for g in range(GROUPS):
            for d in range(NTP):
                keys[g, d * span : (d + 1) * span, :] = pieces[d][g * span : (g + 1) * span, :]
            keys_t[g] = keys[g].T
        acc[...] = jnp.zeros_like(acc)
        spread[...] = jnp.zeros_like(spread)

    maps = jnp.concatenate([vu_ref[h] for h in range(4)], axis=1)
    dqs = []
    for g in range(GROUPS):
        hg = (hg_a, hg_b)[g]
        q4 = jnp.concatenate([q_ref[h][:, g * GQ : (g + 1) * GQ] for h in range(4)], axis=1)
        for h in range(4):
            spread[h * GQ : (h + 1) * GQ, h * VALUE : (h + 1) * VALUE] = hg[
                :, h * VALUE : (h + 1) * VALUE
            ]
        og = mm(maps, spread[...], NT).astype(bf16)
        s = mm(keys[g], q4, NN)
        s = s.reshape(NTP, GSLOTS, PIECE, 4 * GQ) * SCORE_SCALE + bias_ref[g][None, :, None, :]
        s = s.reshape(GROUP_ROWS, 4 * GQ)
        top = jnp.max(s, axis=0, keepdims=True)
        p = jnp.exp(s - top)
        p = p * (1.0 / jnp.sum(p, axis=0, keepdims=True))
        dp = mm(keys[g, :, :LATENT], og, NN)
        delta = jnp.sum(p * dp, axis=0, keepdims=True)
        ds = (p * (dp - delta) * SCORE_SCALE).astype(bf16)
        dqs.append(mm(keys_t[g], ds, NN).astype(bf16))
        acc[g] += mm(ds, q4, NT)
        acc[g, :, :LATENT] += mm(p.astype(bf16), og, NT)
    for h in range(4):
        cols = slice(h * GQ, (h + 1) * GQ)
        dq_ref[h] = jnp.concatenate([dqs[0][:, cols], dqs[1][:, cols]], axis=1)

    @pl.when(step == pl.num_programs(0) - 1)
    def _():
        for d in range(NTP):
            for g in range(GROUPS):
                rows = acc[g, d * span : (d + 1) * span, :].astype(bf16)
                if d < 4:
                    outs[d][g * span : (g + 1) * span, :] = rows
                elif d == 4:
                    outs[4 + g][...] = rows
                else:
                    outs[d + 1][g * span : (g + 1) * span, :] = rows


def attend(pieces, q_t, hg_a, hg_b, vu, bias):
    span = GSLOTS * PIECE
    whole = lambda s: (0, 0)
    rows = [2 * span] * 4 + [span] * 2 + [2 * span] * 3
    out_specs = [pl.BlockSpec((4, WIDTH, QRY_DEV), lambda s: (s, 0, 0))]
    out_specs += [pl.BlockSpec((r, WIDTH), whole) for r in rows]
    out_shape = [jax.ShapeDtypeStruct((HEADS_DEV, WIDTH, QRY_DEV), bf16)]
    out_shape += [jax.ShapeDtypeStruct((r, WIDTH), bf16) for r in rows]
    return pl.pallas_call(
        attend_kernel,
        grid=(HEADS_DEV // 4,),
        in_specs=[pl.BlockSpec(pieces[0].shape, whole)] * NTP
        + [
            pl.BlockSpec((4, WIDTH, QRY_DEV), lambda s: (s, 0, 0)),
            pl.BlockSpec((GQ, 4 * VALUE), lambda s: (0, s)),
            pl.BlockSpec((GQ, 4 * VALUE), lambda s: (0, s)),
            pl.BlockSpec((4, LATENT, VALUE), lambda s: (s, 0, 0)),
            pl.BlockSpec(bias.shape, lambda s: (0, 0, 0)),
        ],
        out_specs=out_specs,
        out_shape=out_shape,
        scratch_shapes=[
            pltpu.VMEM((GROUPS, GROUP_ROWS, WIDTH), bf16),
            pltpu.VMEM((GROUPS, WIDTH, GROUP_ROWS), bf16),
            pltpu.VMEM((GROUPS, GROUP_ROWS, WIDTH), f32),
            pltpu.VMEM((4 * GQ, 4 * VALUE), bf16),
        ],
        compiler_params=params(48),
        cost_estimate=cost(1e10, 1.2e7),
    )(*pieces, q_t, hg_a, hg_b, vu, bias)


def reduce_tp(parts):
    d0, d1, d2, d3, d4a, d4b, d5, d6, d7 = parts
    half = d4a.shape[0]
    up = shift(d4a, "tp", NTP, 1)
    down = shift(d4b, "tp", NTP, -1)
    up = shift(jnp.concatenate([add(d3[:half], up), d3[half:]], axis=0), "tp", NTP, 1)
    down = shift(jnp.concatenate([d5[:half], add(d5[half:], down)], axis=0), "tp", NTP, -1)
    up = shift(add(d2, up), "tp", NTP, 1)
    down = shift(add(d6, down), "tp", NTP, -1)
    up = shift(add(d1, up), "tp", NTP, 1)
    down = shift(add(d7, down), "tp", NTP, -1)
    return d0, up, down


def slots_kernel(chosen, own, up, down, out_ref):
    total = own[...].astype(f32) + up[...].astype(f32) + down[...].astype(f32)
    total = total.astype(bf16)
    out_ref[...] = jnp.zeros_like(out_ref)
    for k in range(SLOTS):
        out_ref[chosen[k]] = total[k * PIECE : (k + 1) * PIECE, :]


def to_slots(chosen, own, up, down):
    return pl.pallas_call(
        slots_kernel,
        in_specs=[smem(), vmem(), vmem(), vmem()],
        out_specs=vmem(),
        out_shape=jax.ShapeDtypeStruct((NCTX, PIECE, WIDTH), bf16),
        compiler_params=params(8),
        cost_estimate=cost(1e6, 2e6),
    )(chosen, own, up, down)


def collect_kernel(ids, got_ref, out_ref):
    out_ref[...] = jnp.zeros_like(out_ref)
    for s in range(NCTX):
        out_ref[ids[s]] += got_ref[s].astype(f32)


def collect(ids, got, blocks):
    return pl.pallas_call(
        collect_kernel,
        in_specs=[smem(), vmem()],
        out_specs=vmem(),
        out_shape=jax.ShapeDtypeStruct((blocks, PIECE, WIDTH), f32),
        compiler_params=params(8),
        cost_estimate=cost(1e6, 2e6),
    )(ids, got)


def shards(
    queries,
    latent_block_cache,
    selected_block_lists,
    output_gradient,
    output_weight,
    adapter_down,
    adapter_up,
    value_up_map,
    saved_head_input,
):
    ctx_axes = ("x", "y", "core")
    blocks_dev = latent_block_cache.shape[0]
    place = jnp.stack(
        [lax.axis_index("x"), lax.axis_index("y"), lax.axis_index("core"), lax.axis_index("tp")]
    ).astype(jnp.int32)

    holder = selected_block_lists // blocks_dev
    local = selected_block_lists - holder * blocks_dev
    every = jnp.arange(NCTX, dtype=jnp.int32)
    hit = holder[:, :, None] == every[None, None, :]
    wanted = jnp.max(jnp.where(hit, local[:, :, None], 0), axis=(0, 1))
    ids = lax.all_to_all(wanted, ctx_axes, split_axis=0, concat_axis=0, tiled=True)

    used = jnp.any(hit.reshape(GROUPS, GQ * hit.shape[1], NCTX), axis=1).astype(jnp.int32)
    rank = jnp.cumsum(used, axis=1)
    slot_hit = (used[:, None, :] == 1) & (
        rank[:, None, :] == jnp.arange(1, GSLOTS + 1, dtype=jnp.int32)[None, :, None]
    )
    chosen = jnp.sum(jnp.where(slot_hit, every[None, None, :], 0), axis=2).reshape(SLOTS)
    holder_groups = holder.reshape(GROUPS, GQ, holder.shape[1])
    picked = jnp.any(
        holder_groups[:, None, :, :] == chosen.reshape(GROUPS, GSLOTS)[:, :, None, None], axis=3
    )
    bias = jnp.where(picked, 0.0, MASKED).astype(f32)
    bias = jnp.concatenate([bias] * 4, axis=2)

    g_t = output_gradient.T
    mine, other, low, w_own = prep(place, g_t, adapter_up, output_weight.T, adapter_down)
    theirs = shift(other, "core", 2, 1)
    w_pair = shift(w_own, "core", 2, 1)

    cache_piece = turn_cache(place, jnp.swapaxes(latent_block_cache, 1, 2))
    rows = adapter_rows(saved_head_input, adapter_down)
    got = lax.all_to_all(
        serve(ids, cache_piece, low, rows), ctx_axes, split_axis=0, concat_axis=0, tiled=True
    )
    pieces = gather_tp(pick(chosen, got, g_t))
    down_part, up_gradient = adapter_grads(place, pieces, saved_head_input)
    down_gradient = lax.psum(down_part, ctx_axes).astype(f32)

    a_own, a_p1, a_m1, a_p2, a_m2, b_own, b_p1, b_m1, b_p2, b_m2 = head_partials(
        place, mine, theirs, w_own, w_pair
    )
    a_minus = shift(a_p1, "x", NX, 1)
    b_minus = shift(b_p1, "y", NY, 1)
    a_plus = shift(a_m1, "x", NX, -1)
    b_plus = shift(b_m1, "y", NY, -1)
    a_last_minus = shift(add(a_p2, a_minus[2:]), "x", NX, 1)
    a_last_plus = shift(add(a_m2, a_plus[:2]), "x", NX, -1)
    b_last_minus = shift(add(b_p2, b_minus[:2]), "y", NY, 1)
    b_last_plus = shift(add(b_m2, b_plus[2:]), "y", NY, -1)
    a_total = jnp.concatenate(
        [add(a_own[:2], a_plus[2:], a_last_minus), add(a_own[2:], a_minus[:2], a_last_plus)], axis=0
    )
    b_total = jnp.concatenate(
        [add(b_own[:2], b_plus[:2], b_last_minus), add(b_own[2:], b_minus[2:], b_last_plus)], axis=0
    )
    hg_a = reduce_second("y", a_total)
    hg_b = reduce_second("x", b_total)

    dq_t, *parts = attend(
        pieces, jnp.transpose(queries, (1, 2, 0)), hg_a, hg_b, value_up_map, bias
    )
    query_grads = jnp.transpose(dq_t, (2, 0, 1))

    own, up, down = reduce_tp(parts)
    returned = lax.all_to_all(
        to_slots(chosen, own, up, down), ctx_axes, split_axis=0, concat_axis=0, tiled=True
    )
    cache_grads = collect(ids, returned, blocks_dev)
    return (query_grads, cache_grads, down_gradient, up_gradient)


def solution(mesh):
    split = Mesh(mesh.devices.reshape(NX, NY, NCORE, NTP), ("x", "y", "core", "tp"))
    ctx = ("x", "y", "core")
    placed = (
        P(ctx, "tp", None),
        P(ctx, None, None),
        P(ctx, None),
        P(None, ctx),
        P("tp", ctx),
        P(None, "tp"),
        P(None, ctx),
        P("tp", None, None),
        P(ctx, "tp"),
    )
    return jax.shard_map(
        shards,
        mesh=split,
        in_specs=placed,
        out_specs=(P(ctx, "tp", None), P(ctx, "tp", None), P(None, "tp"), P(None, ctx)),
        check_vma=False,
    )
```

time: 499 us -> 358 us (0.72)
  local copies, waits for them, and re-layouts: 105 us -> 17.8 us
  starting transfers between devices: 12.2 us -> 88.4 us
  blocking collectives: 70 us -> 0 us
  matrix products: 66.5 us -> 0 us
  Pallas kernels: 0 us -> 49.6 us
  other arithmetic: 43.8 us -> 10.1 us
  waiting for transfers between devices: 179 us -> 171 us
    psum x1, waiting for transfers between devices: 0.01 us -> 112 us  [shards(): down_gradient = lax.psum(down_part, ctx_axes).astype(f32)]
    all_to_all x2 -> x3, waiting for transfers between devices: 107 us -> 4.29 us  [the longest x1 4.29 us: shards(): lax.all_to_all(wanted, ctx_axes, split_axis=0, concat_axis=0, tiled=True)]
    dot_general x18 -> x0, matrix products: 66.5 us -> none  [the longest x1 18.1 us: shards(): jnp.dot(adapter_low, down_single_float, precision=lax.Precision.HIGHEST)]
    ppermute x0 -> x33, starting transfers between devices: none -> 66.5 us  [shift(): lax.ppermute(value, axis, [(i, (i + by) % size) for i in range(size)])]
    ppermute x0 -> x33, waiting for transfers between devices: none -> 55.3 us  [shift(): lax.ppermute(value, axis, [(i, (i + by) % size) for i in range(size)])]
    pallas_call x0 -> x10, Pallas kernels: none -> 49.6 us  [the longest x1 20.2 us: attend(): pl.pallas_call(attend_kernel, grid=(HEADS_DEV // 4,), in_specs=[pl.BlockS...]
    reduce_scatter x1 -> x0, waiting for transfers between devices: 41.6 us -> none  [shards(): lax.psum_scatter(owned_grads.astype(jnp.bfloat16), 'tp', scatter_dimensio...]
    psum x1 -> x0, blocking collectives: 30.2 us -> none  [shards(): row_total_part = lax.psum(row_portion, 'tp')]
  transfers between devices with their start and end apart: 5 -> 37, of which waited for: 4 -> 17; matrix products, arithmetic and copies ran while one was open for 15% -> 3% of each run, Pallas kernels for 0% -> 5%
where the time goes in v1:
time: 358 us; the launch traced here: 352 us
  waiting for transfers between devices  171 us (48%)
  starting transfers between devices  88.4 us (25%)
  Pallas kernels  49.6 us (14%)
  local copies, waits for them, and re-layouts  17.8 us (5%)
  between operations  14.7 us (4%)
  other arithmetic  10.1 us (3%)
    psum x1, waiting for transfers between devices, shards(): down_gradient = lax.psum(down_part, ctx_axes).astype(f32)  112 us
    ppermute x33, starting transfers between devices, shift(): lax.ppermute(value, axis, [(i, (i + by) % size) for i in range(size)])  66.5 us
    ppermute x33, waiting for transfers between devices, shift(): lax.ppermute(value, axis, [(i, (i + by) % size) for i in range(size)])  55.3 us
    pallas_call x1, Pallas kernels, attend(): pl.pallas_call(attend_kernel, grid=(HEADS_DEV // 4,), in_specs=[pl.BlockS...  20.2 us
    unnamed x52, local copies, waits for them, and re-layouts  15.9 us
    pallas_call x1, Pallas kernels, head_partials(): pl.pallas_call(head_kernel, grid_spec=pltpu.PrefetchScalarGridSpec(num_sc...  12.3 us
    all_to_all x1, starting transfers between devices, shards(): lax.all_to_all(to_slots(chosen, own, up, down), ctx_axes, split_axis=0, c...  9.23 us
    pallas_call x1, Pallas kernels, prep(): pl.pallas_call(prep_kernel, grid_spec=pltpu.PrefetchScalarGridSpec(num_sc...  8 us
  transfers between devices with their start and end apart: 37, of which 17 were waited for; matrix products, arithmetic and copies ran while one was open for 3% of the time, Pallas kernels for 5%

profile of v1, /device:TPU:2, one launch (start us, length us, event | category | flops | bytes accessed | tf_op | source)
XLA Modules:
  0.0 351.9 jit_solution(14277258426655604267)
XLA Ops:
  7.3 1.5 copy-done
  8.8 1.2 copy-done.8
  9.9 0.9 copy-done.15
  11.6 8.0 %shard_map.121 = (bf16[16,128,256]{2,1,0:T(8,128)(2,1)S(1)}, bf16[16,128,256]{2,1,0:T(8,128)(2,1)}, bf16[32,16,128]{2,1,0:T(8,128)(2,1)S(1)}, bf16[256,2048]{1,0:T(8,128)(2,1)}) custom-call(s32[4]{0:T(128)S(1)} %pad_add_fusion.place, bf16[224,4096]{1,0:T(8,128)(2,1)S(1)} %bitcast.68, bf16[32,224]{1,0:T(8,128)(2,1)S(1)} %copy-done.18, ...), custom_call_target="tpu_custom_call" | custom-call | flops 100000000 | bytes 6000000 | tf_op jit(solution)/shard_map/pallas_call | solution.py:86
  20.2 1.0 copy-done.21
  22.6 7.6 %all-to-all-start = ((s32[32,1,1]{2,1,0:T(1,128)}), s32[32,1,1]{2,1,0:T(1,128)S(1)}, u32[]{:S(2)}, u32[]{:S(2)}) async-start(s32[32,1,1]{2,1,0:T(1,128)} %copy.32), calls=%async_computation | async-start | bytes 32768 | tf_op jit(solution)/shard_map/all_to_all | solution.py:529
  30.7 1.3 shard_map.120.cache_ref
  32.0 4.3 %all-to-all-done = s32[32,1,1]{2,1,0:T(1,128)S(1)} async-done(((s32[32,1,1]{2,1,0:T(1,128)}), s32[32,1,1]{2,1,0:T(1,128)S(1)}, u32[]{:S(2)}, u32[]{:S(2)}) %all-to-all-start) | async-done | bytes 160 | tf_op jit(solution)/shard_map/all_to_all | solution.py:529
  37.0 0.9 copy-done.17
  37.9 1.6 shard_map.123
  39.5 5.0 %all-to-all-start.1 = ((bf16[32,16,896]{2,1,0:T(8,128)(2,1)}), bf16[32,16,896]{2,1,0:T(8,128)(2,1)S(1)}, u32[]{:S(2)}, u32[]{:S(2)}) async-start(bf16[32,16,896]{2,1,0:T(8,128)(2,1)} %shard_map.123), calls=%async_computation.1 | async-start | bytes 1835008 | tf_op jit(solution)/shard_map/all_to_all | solution.py:551
  44.7 1.2 copy-done.22
  45.9 12.3 %shard_map.125 = (bf16[4,64,2048]{2,1,0:T(8,128)(2,1)S(1)}, bf16[4,64,2048]{2,1,0:T(8,128)(2,1)}, bf16[4,64,2048]{2,1,0:T(8,128)(2,1)}, bf16[2,64,2048]{2,1,0:T(...) custom-call(s32[4]{0:T(128)S(1)} %pad_add_fusion.place, ...), custom_call_target="tpu_custom_call" | custom-call | flops 4300000256 | bytes 13000000 | tf_op jit(solution)/shard_map/pallas_call | solution.py:190
  58.2 1.0 copy-done.4
  59.2 1.0 copy-done.6
  60.2 0.8 copy-done.9
  61.1 0.9 copy-done.11
  63.5 1.0 copy-done.19
  64.5 1.0 copy-done.20
  65.5 1.5 collective-permute-start.10
  68.1 1.2 shard_map.124.refs_0_
  69.4 5.9 %collective-permute-start = (bf16[208,576]{1,0:T(8,128)(2,1)S(1)}, bf16[208,576]{1,0:T(8,128)(2,1)S(1)}, u32[]{:S(2)}, u32[]{:S(2)}) collective-permute-start(bf16[208,576]{1,0:T(8,128)(2,1)S(1)} %shard_map.124.refs_0_), channel_id=1, source_target_pairs={{0,7},{1,0},{2,1},{3,2},{4,3},{5,4},{6,5},{7,6},{8,15},{9,8},{10,9... | collective-permute-start | bytes 718856 | tf_op jit(solution)/shard_map/ppermute | solution.py:205
  75.3 5.7 %collective-permute-done.refs_1_ = bf16[208,576]{1,0:T(8,128)(2,1)S(1)} collective-permute-done((bf16[208,576]{1,0:T(8,128)(2,1)S(1)}, bf16[208,576]{1,0:T(8,128)(2,1)S(1)}, u32[]{:S(2)}, u32[]{:S(2)}) %collective-permute-start) | collective-permute-done | bytes 239648 | tf_op jit(solution)/shard_map/ppermute | solution.py:205
  81.0 3.7 %collective-permute-start.1 = (bf16[208,576]{1,0:T(8,128)(2,1)S(1)}, bf16[208,576]{1,0:T(8,128)(2,1)S(1)}, u32[]{:S(2)}, u32[]{:S(2)}) collective-permute-start(bf16[208,576]{1,0:T(8,128)(2,1)S(1)} %collective-permute-done.refs_1_), channel_id=1, source_target_pairs={{0,7},{1,0},{2,1},{3,2},{4,3},{5,4},{6,5},{7,6},{8,15},{9,8},{10,9... | collective-permute-start | bytes 718856 | tf_op jit(solution)/shard_map/ppermute | solution.py:205
  86.8 2.7 collective-permute-done.1.refs_2_
  89.5 3.7 %collective-permute-start.2 = (bf16[208,576]{1,0:T(8,128)(2,1)S(1)}, bf16[208,576]{1,0:T(8,128)(2,1)S(1)}, u32[]{:S(2)}, u32[]{:S(2)}) collective-permute-start(bf16[208,576]{1,0:T(8,128)(2,1)S(1)} %collective-permute-done.1.refs_2_), channel_id=1, source_target_pairs={{0,7},{1,0},{2,1},{3,2},{4,3},{5,4},{6,5},{7,6},{8,15},{9,8},{10,9... | collective-permute-start | bytes 718856 | tf_op jit(solution)/shard_map/ppermute | solution.py:205
  93.2 1.7 collective-permute-start.18
  95.0 2.6 collective-permute-start.17
  97.6 3.2 collective-permute-start.3
  100.8 1.4 add_convert_fusion.7
  102.2 6.6 %collective-permute-done.9 = bf16[4,64,2048]{2,1,0:T(8,128)(2,1)} collective-permute-done((bf16[4,64,2048]{2,1,0:T(8,128)(2,1)}, bf16[4,64,2048]{2,1,0:T(8,128)(2,1)}, u32[]{:S(2)}, u32[]{:S(2)}) %collective-permute-start.9) | collective-permute-done | bytes 1048608 | tf_op jit(solution)/shard_map/ppermute | solution.py:205
  108.8 1.2 collective-permute-start.11
  110.0 1.4 add_convert_fusion.5
  111.4 6.3 %collective-permute-done.18 = bf16[4,64,2048]{2,1,0:T(8,128)(2,1)S(1)} collective-permute-done((bf16[4,64,2048]{2,1,0:T(8,128)(2,1)}, bf16[4,64,2048]{2,1,0:T(8,128)(2,1)S(1)}, u32[]{:S(2)}, u32[]{:S(2)}) %collective-permute-start.18) | collective-permute-done | bytes 1048608 | tf_op jit(solution)/shard_map/ppermute | solution.py:205
  117.7 0.8 collective-permute-start.12
  119.4 1.0 collective-permute-done.11
  120.4 2.7 collective-permute-start.20
  123.1 5.3 %collective-permute-done.12 = bf16[2,64,2048]{2,1,0:T(8,128)(2,1)S(1)} collective-permute-done((bf16[2,64,2048]{2,1,0:T(8,128)(2,1)S(1)}, bf16[2,64,2048]{2,1,0:T(8,128)(2,1)S(1)}, u32[]{:S(2)}, u32[]{:S(2)}) %collective-permute-start.12) | collective-permute-done | bytes 524320 | tf_op jit(solution)/shard_map/ppermute | solution.py:205
  128.4 1.7 add_convert_fusion.6
  131.1 2.9 collective-permute-start.13
  134.7 1.3 collective-permute-start.22
  135.9 1.9 collective-permute-done.13
  137.9 1.6 collective-permute-start.21
  139.5 4.8 %collective-permute-done.21 = bf16[64,2048]{1,0:T(8,128)(2,1)S(1)} collective-permute-done((bf16[64,2048]{1,0:T(8,128)(2,1)S(1)}, bf16[64,2048]{1,0:T(8,128)(2,1)S(1)}, u32[]{:S(2)}, u32[]{:S(2)}) %collective-permute-start.21) | collective-permute-done | bytes 262176 | tf_op jit(solution)/shard_map/ppermute | solution.py:205
  144.3 5.1 %collective-permute-start.16 = (bf16[32,2048]{1,0:T(8,128)(2,1)S(1)}, bf16[32,2048]{1,0:T(8,128)(2,1)S(1)}, u32[]{:S(2)}, u32[]{:S(2)}) collective-permute-start(bf16[32,2048]{1,0:T(8,128)(2,1)S(1)} %fusion.6), channel_id=1, source_target_pairs={{0,48},{16,0},{32,16},{48,32},{1,49},{17,1},{33,17},{49,33},{2,50}... | collective-permute-start | bytes 393224 | tf_op jit(solution)/shard_map/ppermute | solution.py:205
  149.4 1.7 collective-permute-start.24
  152.0 9.8 %collective-permute-start.15 = (bf16[32,2048]{1,0:T(8,128)(2,1)S(1)}, bf16[32,2048]{1,0:T(8,128)(2,1)S(1)}, u32[]{:S(2)}, u32[]{:S(2)}) collective-permute-start(bf16[32,2048]{1,0:T(8,128)(2,1)S(1)} %get-tuple-element.62), channel_id=1, source_target_pairs={{0,16},{16,32},{32,48},{48,0},{1,17},{17,33},{33,49},{49,1},{2,18}... | collective-permute-start | bytes 393224 | tf_op jit(solution)/shard_map/ppermute | solution.py:205
  161.9 1.0 collective-permute-start.23
  162.9 5.5 %collective-permute-done.15 = bf16[32,2048]{1,0:T(8,128)(2,1)S(1)} collective-permute-done((bf16[32,2048]{1,0:T(8,128)(2,1)S(1)}, bf16[32,2048]{1,0:T(8,128)(2,1)S(1)}, u32[]{:S(2)}, u32[]{:S(2)}) %collective-permute-start.15) | collective-permute-done | bytes 131104 | tf_op jit(solution)/shard_map/ppermute | solution.py:205
  168.5 20.2 %shard_map.126 = (bf16[16,576,128]{2,1,0:T(8,128)(2,1)}, bf16[192,576]{1,0:T(8,128)(2,1)S(1)}, bf16[192,576]{1,0:T(8,128)(2,1)S(1)}, bf16[192,576]{1,0:T(8,128)(...) custom-call(bf16[208,576]{1,0:T(8,128)(2,1)S(1)} %shard_map.124.refs, ...), custom_call_target="tpu_custom_call" | custom-call | flops 10000000000 | bytes 12000000 | tf_op jit(solution)/shard_map/pallas_call | solution.py:433
  188.8 3.3 collective-permute-start.29
  192.1 2.7 collective-permute-done.25
  195.1 3.3 collective-permute-start.30
  198.4 4.1 %collective-permute-done.26 = bf16[192,576]{1,0:T(8,128)(2,1)S(1)} collective-permute-done((bf16[192,576]{1,0:T(8,128)(2,1)S(1)}, bf16[192,576]{1,0:T(8,128)(2,1)S(1)}, u32[]{:S(2)}, u32[]{:S(2)}) %collective-permute-start.26) | collective-permute-done | bytes 221216 | tf_op jit(solution)/shard_map/ppermute | solution.py:205
  202.7 3.6 %collective-permute-start.31 = (bf16[192,576]{1,0:T(8,128)(2,1)S(1)}, bf16[192,576]{1,0:T(8,128)(2,1)S(1)}, u32[]{:S(2)}, u32[]{:S(2)}) collective-permute-start(bf16[192,576]{1,0:T(8,128)(2,1)S(1)} %add_convert_fusion.9), channel_id=1, source_target_pairs={{0,7},{1,0},{2,1},{3,2},{4,3},{5,4},{6,5},{7,6},{8,15},{9,8},{10,9... | collective-permute-start | bytes 663560 | tf_op jit(solution)/shard_map/ppermute | solution.py:205
  206.3 3.7 %collective-permute-done.27 = bf16[192,576]{1,0:T(8,128)(2,1)S(1)} collective-permute-done((bf16[192,576]{1,0:T(8,128)(2,1)S(1)}, bf16[192,576]{1,0:T(8,128)(2,1)S(1)}, u32[]{:S(2)}, u32[]{:S(2)}) %collective-permute-start.27) | collective-permute-done | bytes 221216 | tf_op jit(solution)/shard_map/ppermute | solution.py:205
  210.3 3.6 %collective-permute-start.32 = (bf16[192,576]{1,0:T(8,128)(2,1)S(1)}, bf16[192,576]{1,0:T(8,128)(2,1)S(1)}, u32[]{:S(2)}, u32[]{:S(2)}) collective-permute-start(bf16[192,576]{1,0:T(8,128)(2,1)S(1)} %add_convert_fusion.8), channel_id=1, source_target_pairs={{0,7},{1,0},{2,1},{3,2},{4,3},{5,4},{6,5},{7,6},{8,15},{9,8},{10,9... | collective-permute-start | bytes 663560 | tf_op jit(solution)/shard_map/ppermute | solution.py:205
  213.9 3.7 %collective-permute-done.28.up = bf16[192,576]{1,0:T(8,128)(2,1)S(1)} collective-permute-done((bf16[192,576]{1,0:T(8,128)(2,1)S(1)}, bf16[192,576]{1,0:T(8,128)(2,1)S(1)}, u32[]{:S(2)}, u32[]{:S(2)}) %collective-permute-start.28) | collective-permute-done | bytes 221216 | tf_op jit(solution)/shard_map/ppermute | solution.py:205
  217.6 1.5 shard_map.127
  219.1 9.2 %all-to-all-start.2 = ((bf16[32,16,576]{2,1,0:T(8,128)(2,1)}), bf16[32,16,576]{2,1,0:T(8,128)(2,1)S(1)}, u32[]{:S(2)}, u32[]{:S(2)}) async-start(bf16[32,16,576]{2,1,0:T(8,128)(2,1)} %shard_map.127), calls=%async_computation.2 | async-start | bytes 1310720 | tf_op jit(solution)/shard_map/all_to_all | solution.py:584
  228.4 1.6 shard_map.129
  230.0 111.6 %all-reduce.2.cloned.1.call-done = bf16[32,2048]{1,0:T(8,128)(2,1)} async-done(((bf16[32,2048]{1,0:T(8,128)(2,1)}), bf16[32,2048]{1,0:T(8,128)(2,1)}) %all-reduce.2.cloned.1.call-update) | async-done | bytes 131088 | tf_op jit(solution)/shard_map/psum | solution.py:556
  341.6 1.6 convert_element_type.343
  343.2 1.6 shard_map.128
  (125 shorter events, 13.4 us)
Async XLA Ops:
  7.2 14.5 %copy-start.25 = (s32[128,4]{0,1:T(4,128)S(1)}, s32[128,4]{0,1:T(4,128)}, u32[]{:S(2)}) copy-start(s32[128,4]{0,1:T(4,128)} %param.11) | copy-start | bytes 6148
  7.3 1.5 copy-start
  8.8 1.2 copy-start.8
  9.9 0.9 copy-start.15
  10.8 0.7 copy-start.18
  11.6 18.8 %copy-start.3 = (bf16[128,2048]{1,0:T(8,128)(2,1)S(1)}, bf16[128,2048]{1,0:T(8,128)(2,1)}, u32[]{:S(2)}) copy-start(bf16[128,2048]{1,0:T(8,128)(2,1)} %refs_8_.1) | copy-start | bytes 1572868
  11.6 19.1 %copy-start.2 = (bf16[16,128,576]{1,2,0:T(8,128)(2,1)S(1)}, bf16[16,128,576]{1,2,0:T(8,128)(2,1)}, u32[]{:S(2)}) copy-start(bf16[16,128,576]{1,2,0:T(8,128)(2,1)} %param.10) | copy-start | bytes 7077892
  19.6 0.7 copy-start.16
  20.2 1.0 copy-start.21
  21.2 23.4 %collective-permute-start.7 = (bf16[16,128,256]{2,1,0:T(8,128)(2,1)}, bf16[16,128,256]{2,1,0:T(8,128)(2,1)}, u32[]{:S(2)}, u32[]{:S(2)}) collective-permute-start(bf16[16,128,256]{2,1,0:T(8,128)(2,1)} %get-tuple-element.32), channel_id=1, source_target_pairs={{0,8},{8,0},{1,9},{9,1},{2,10},{10,2},{3,11},{11,3},{4,12},{12,4},... | collective-permute-start | bytes 3145736 | tf_op jit(solution)/shard_map/ppermute | solution.py:205
  21.2 23.4 %collective-permute-start.8 = (bf16[256,2048]{1,0:T(8,128)(2,1)}, bf16[256,2048]{1,0:T(8,128)(2,1)}, u32[]{:S(2)}, u32[]{:S(2)}) collective-permute-start(bf16[256,2048]{1,0:T(8,128)(2,1)} %get-tuple-element.33.w_own), channel_id=1, source_target_pairs={{0,8},{8,0},{1,9},{9,1},{2,10},{10,2},{3,11},{11,3},{4,12},{12,4},... | collective-permute-start | bytes 3145736 | tf_op jit(solution)/shard_map/ppermute | solution.py:205
  21.7 17.7 %copy-start.23 = (s32[128,4]{0,1:T(4,128)}, s32[128,4]{0,1:T(4,128)S(1)}, u32[]{:S(2)}) copy-start(s32[128,4]{0,1:T(4,128)S(1)} %get-tuple-element.71) | copy-start | bytes 6148
  22.6 13.7 %all-to-all-start = ((s32[32,1,1]{2,1,0:T(1,128)}), s32[32,1,1]{2,1,0:T(1,128)S(1)}, u32[]{:S(2)}, u32[]{:S(2)}) async-start(s32[32,1,1]{2,1,0:T(1,128)} %copy.32), calls=%async_computation | async-start | bytes 32768 | tf_op jit(solution)/shard_map/all_to_all | solution.py:529
  37.0 0.9 copy-start.17
  39.5 28.7 %all-to-all-start.1 = ((bf16[32,16,896]{2,1,0:T(8,128)(2,1)}), bf16[32,16,896]{2,1,0:T(8,128)(2,1)S(1)}, u32[]{:S(2)}, u32[]{:S(2)}) async-start(bf16[32,16,896]{2,1,0:T(8,128)(2,1)} %shard_map.123), calls=%async_computation.1 | async-start | bytes 1835008 | tf_op jit(solution)/shard_map/all_to_all | solution.py:551
  44.6 1.2 copy-start.22
  45.9 22.2 %copy-start.1 = (bf16[4096,224]{0,1:T(8,128)(2,1)S(1)}, bf16[4096,224]{0,1:T(8,128)(2,1)}, u32[]{:S(2)}) copy-start(bf16[4096,224]{0,1:T(8,128)(2,1)} %param.12) | copy-start | bytes 5505028
  58.2 1.0 copy-start.4
  59.2 1.0 copy-start.6
  60.2 0.8 copy-start.9
  61.0 0.9 copy-start.11
  61.9 0.8 copy-start.13
  62.7 0.8 copy-start.14
  63.5 1.0 copy-start.19
  64.5 1.0 copy-start.20
  65.5 32.1 %collective-permute-start.10 = (bf16[4,64,2048]{2,1,0:T(8,128)(2,1)}, bf16[4,64,2048]{2,1,0:T(8,128)(2,1)}, u32[]{:S(2)}, u32[]{:S(2)}) collective-permute-start(bf16[4,64,2048]{2,1,0:T(8,128)(2,1)} %get-tuple-element.37), channel_id=1, source_target_pairs={{0,64},{64,128},{128,192},{192,0},{1,65},{65,129},{129,193},{193,1... | collective-permute-start | bytes 3145736 | tf_op jit(solution)/shard_map/ppermute | solution.py:205
  67.5 0.6 copy-start.24
  69.3 49.2 %copy-start.12 = (bf16[2,64,2048]{2,1,0:T(8,128)(2,1)S(1)}, bf16[2,64,2048]{2,1,0:T(8,128)(2,1)}, u32[]{:S(2)}) copy-start(bf16[2,64,2048]{2,1,0:T(8,128)(2,1)} %copy-done.11) | copy-start | bytes 1572868
  69.4 11.6 %collective-permute-start = (bf16[208,576]{1,0:T(8,128)(2,1)S(1)}, bf16[208,576]{1,0:T(8,128)(2,1)S(1)}, u32[]{:S(2)}, u32[]{:S(2)}) collective-permute-start(bf16[208,576]{1,0:T(8,128)(2,1)S(1)} %shard_map.124.refs_0_), channel_id=1, source_target_pairs={{0,7},{1,0},{2,1},{3,2},{4,3},{5,4},{6,5},{7,6},{8,15},{9,8},{10,9... | collective-permute-start | bytes 718856 | tf_op jit(solution)/shard_map/ppermute | solution.py:205
  75.3 11.4 %collective-permute-start.4 = (bf16[208,576]{1,0:T(8,128)(2,1)S(1)}, bf16[208,576]{1,0:T(8,128)(2,1)S(1)}, u32[]{:S(2)}, u32[]{:S(2)}) collective-permute-start(bf16[208,576]{1,0:T(8,128)(2,1)S(1)} %shard_map.124.refs_0_), channel_id=1, source_target_pairs={{0,1},{1,2},{2,3},{3,4},{4,5},{5,6},{6,7},{7,0},{8,9},{9,10},{10,1... | collective-permute-start | bytes 718856 | tf_op jit(solution)/shard_map/ppermute | solution.py:205
  81.0 8.5 %collective-permute-start.1 = (bf16[208,576]{1,0:T(8,128)(2,1)S(1)}, bf16[208,576]{1,0:T(8,128)(2,1)S(1)}, u32[]{:S(2)}, u32[]{:S(2)}) collective-permute-start(bf16[208,576]{1,0:T(8,128)(2,1)S(1)} %collective-permute-done.refs_1_), channel_id=1, source_target_pairs={{0,7},{1,0},{2,1},{3,2},{4,3},{5,4},{6,5},{7,6},{8,15},{9,8},{10,9... | collective-permute-start | bytes 718856 | tf_op jit(solution)/shard_map/ppermute | solution.py:205
  84.7 24.1 %collective-permute-start.9 = (bf16[4,64,2048]{2,1,0:T(8,128)(2,1)}, bf16[4,64,2048]{2,1,0:T(8,128)(2,1)}, u32[]{:S(2)}, u32[]{:S(2)}) collective-permute-start(bf16[4,64,2048]{2,1,0:T(8,128)(2,1)} %get-tuple-element.35), channel_id=1, source_target_pairs={{0,192},{64,0},{128,64},{192,128},{1,193},{65,1},{129,65},{193,129... | collective-permute-start | bytes 3145736 | tf_op jit(solution)/shard_map/ppermute | solution.py:205
  86.7 8.3 %collective-permute-start.5 = (bf16[208,576]{1,0:T(8,128)(2,1)S(1)}, bf16[208,576]{1,0:T(8,128)(2,1)S(1)}, u32[]{:S(2)}, u32[]{:S(2)}) collective-permute-start(bf16[208,576]{1,0:T(8,128)(2,1)S(1)} %collective-permute-done.4.refs_7_), channel_id=1, source_target_pairs={{0,1},{1,2},{2,3},{3,4},{4,5},{5,6},{6,7},{7,0},{8,9},{9,10},{10,1... | collective-permute-start | bytes 718856 | tf_op jit(solution)/shard_map/ppermute | solution.py:205
  89.5 8.1 %collective-permute-start.2 = (bf16[208,576]{1,0:T(8,128)(2,1)S(1)}, bf16[208,576]{1,0:T(8,128)(2,1)S(1)}, u32[]{:S(2)}, u32[]{:S(2)}) collective-permute-start(bf16[208,576]{1,0:T(8,128)(2,1)S(1)} %collective-permute-done.1.refs_2_), channel_id=1, source_target_pairs={{0,7},{1,0},{2,1},{3,2},{4,3},{5,4},{6,5},{7,6},{8,15},{9,8},{10,9... | collective-permute-start | bytes 718856 | tf_op jit(solution)/shard_map/ppermute | solution.py:205
  93.2 24.5 %collective-permute-start.18 = (bf16[4,64,2048]{2,1,0:T(8,128)(2,1)}, bf16[4,64,2048]{2,1,0:T(8,128)(2,1)S(1)}, u32[]{:S(2)}, u32[]{:S(2)}) collective-permute-start(bf16[4,64,2048]{2,1,0:T(8,128)(2,1)} %copy-done.20), channel_id=1, source_target_pairs={{0,16},{16,32},{32,48},{48,0},{1,17},{17,33},{33,49},{49,1},{2,18}... | collective-permute-start | bytes 3145736 | tf_op jit(solution)/shard_map/ppermute | solution.py:205
  95.0 23.7 %collective-permute-start.17 = (bf16[4,64,2048]{2,1,0:T(8,128)(2,1)}, bf16[4,64,2048]{2,1,0:T(8,128)(2,1)S(1)}, u32[]{:S(2)}, u32[]{:S(2)}) collective-permute-start(bf16[4,64,2048]{2,1,0:T(8,128)(2,1)} %copy-done.19), channel_id=1, source_target_pairs={{0,48},{16,0},{32,16},{48,32},{1,49},{17,1},{33,17},{49,33},{2,50}... | collective-permute-start | bytes 3145736 | tf_op jit(solution)/shard_map/ppermute | solution.py:205
  97.6 71.0 %collective-permute-start.6 = (bf16[208,576]{1,0:T(8,128)(2,1)S(1)}, bf16[208,576]{1,0:T(8,128)(2,1)S(1)}, u32[]{:S(2)}, u32[]{:S(2)}) collective-permute-start(bf16[208,576]{1,0:T(8,128)(2,1)S(1)} %collective-permute-done.5.refs_6_), channel_id=1, source_target_pairs={{0,1},{1,2},{2,3},{3,4},{4,5},{5,6},{6,7},{7,0},{8,9},{9,10},{10,1... | collective-permute-start | bytes 718856 | tf_op jit(solution)/shard_map/ppermute | solution.py:205
  97.6 71.0 %collective-permute-start.3 = (bf16[208,576]{1,0:T(8,128)(2,1)S(1)}, bf16[208,576]{1,0:T(8,128)(2,1)S(1)}, u32[]{:S(2)}, u32[]{:S(2)}) collective-permute-start(bf16[208,576]{1,0:T(8,128)(2,1)S(1)} %collective-permute-done.2.refs_3_), channel_id=1, source_target_pairs={{0,7},{1,0},{2,1},{3,2},{4,3},{5,4},{6,5},{7,6},{8,15},{9,8},{10,9... | collective-permute-start | bytes 718856 | tf_op jit(solution)/shard_map/ppermute | solution.py:205
  100.8 18.5 %copy-start.10 = (bf16[2,64,2048]{2,1,0:T(8,128)(2,1)S(1)}, bf16[2,64,2048]{2,1,0:T(8,128)(2,1)}, u32[]{:S(2)}) copy-start(bf16[2,64,2048]{2,1,0:T(8,128)(2,1)} %copy-done.9) | copy-start | bytes 1572868
  108.8 11.6 %collective-permute-start.11 = (bf16[2,64,2048]{2,1,0:T(8,128)(2,1)S(1)}, bf16[2,64,2048]{2,1,0:T(8,128)(2,1)S(1)}, u32[]{:S(2)}, u32[]{:S(2)}) collective-permute-start(bf16[2,64,2048]{2,1,0:T(8,128)(2,1)S(1)} %add_convert_fusion.7), channel_id=1, source_target_pairs={{0,64},{64,128},{128,192},{192,0},{1,65},{65,129},{129,193},{193,1... | collective-permute-start | bytes 1572872 | tf_op jit(solution)/shard_map/ppermute | solution.py:205
  110.0 18.4 %copy-start.7 = (bf16[4,64,2048]{2,1,0:T(8,128)(2,1)S(1)}, bf16[4,64,2048]{2,1,0:T(8,128)(2,1)}, u32[]{:S(2)}) copy-start(bf16[4,64,2048]{2,1,0:T(8,128)(2,1)} %copy-done.6) | copy-start | bytes 3145732
  117.7 10.7 %collective-permute-start.12 = (bf16[2,64,2048]{2,1,0:T(8,128)(2,1)S(1)}, bf16[2,64,2048]{2,1,0:T(8,128)(2,1)S(1)}, u32[]{:S(2)}, u32[]{:S(2)}) collective-permute-start(bf16[2,64,2048]{2,1,0:T(8,128)(2,1)S(1)} %add_convert_fusion.5), channel_id=1, source_target_pairs={{0,192},{64,0},{128,64},{192,128},{1,193},{65,1},{129,65},{193,129... | collective-permute-start | bytes 1572872 | tf_op jit(solution)/shard_map/ppermute | solution.py:205
  118.7 12.4 %collective-permute-start.19 = (bf16[2,64,2048]{2,1,0:T(8,128)(2,1)S(1)}, bf16[2,64,2048]{2,1,0:T(8,128)(2,1)S(1)}, u32[]{:S(2)}, u32[]{:S(2)}) collective-permute-start(bf16[2,64,2048]{2,1,0:T(8,128)(2,1)S(1)} %add_convert_fusion.3), channel_id=1, source_target_pairs={{0,16},{16,32},{32,48},{48,0},{1,17},{17,33},{33,49},{49,1},{2,18}... | collective-permute-start | bytes 1572872 | tf_op jit(solution)/shard_map/ppermute | solution.py:205
  120.4 13.6 %collective-permute-start.20 = (bf16[2,64,2048]{2,1,0:T(8,128)(2,1)S(1)}, bf16[2,64,2048]{2,1,0:T(8,128)(2,1)S(1)}, u32[]{:S(2)}, u32[]{:S(2)}) collective-permute-start(bf16[2,64,2048]{2,1,0:T(8,128)(2,1)S(1)} %add_convert_fusion.1), channel_id=1, source_target_pairs={{0,48},{16,0},{32,16},{48,32},{1,49},{17,1},{33,17},{49,33},{2,50}... | collective-permute-start | bytes 1572872 | tf_op jit(solution)/shard_map/ppermute | solution.py:205
  128.4 5.6 %copy-start.5 = (bf16[4,64,2048]{2,1,0:T(8,128)(2,1)S(1)}, bf16[4,64,2048]{2,1,0:T(8,128)(2,1)}, u32[]{:S(2)}) copy-start(bf16[4,64,2048]{2,1,0:T(8,128)(2,1)} %copy-done.4) | copy-start | bytes 3145732
  130.2 19.2 %collective-permute-start.14 = (bf16[64,2048]{1,0:T(8,128)(2,1)S(1)}, bf16[64,2048]{1,0:T(8,128)(2,1)S(1)}, u32[]{:S(2)}, u32[]{:S(2)}) collective-permute-start(bf16[64,2048]{1,0:T(8,128)(2,1)S(1)} %pad_maximum_fusion.1), channel_id=1, source_target_pairs={{0,16},{16,32},{32,48},{48,0},{1,17},{17,33},{33,49},{49,1},{2,18}... | collective-permute-start | bytes 786440 | tf_op jit(solution)/shard_map/ppermute | solution.py:205
  131.1 6.8 %collective-permute-start.13 = (bf16[64,2048]{1,0:T(8,128)(2,1)S(1)}, bf16[64,2048]{1,0:T(8,128)(2,1)S(1)}, u32[]{:S(2)}, u32[]{:S(2)}) collective-permute-start(bf16[64,2048]{1,0:T(8,128)(2,1)S(1)} %pad_maximum_fusion), channel_id=1, source_target_pairs={{0,48},{16,0},{32,16},{48,32},{1,49},{17,1},{33,17},{49,33},{2,50}... | collective-permute-start | bytes 786440 | tf_op jit(solution)/shard_map/ppermute | solution.py:205
  134.7 27.1 %collective-permute-start.22 = (bf16[64,2048]{1,0:T(8,128)(2,1)S(1)}, bf16[64,2048]{1,0:T(8,128)(2,1)S(1)}, u32[]{:S(2)}, u32[]{:S(2)}) collective-permute-start(bf16[64,2048]{1,0:T(8,128)(2,1)S(1)} %pad_maximum_fusion.4), channel_id=1, source_target_pairs={{0,64},{64,128},{128,192},{192,0},{1,65},{65,129},{129,193},{193,1... | collective-permute-start | bytes 786440 | tf_op jit(solution)/shard_map/ppermute | solution.py:205
  137.9 6.4 %collective-permute-start.21 = (bf16[64,2048]{1,0:T(8,128)(2,1)S(1)}, bf16[64,2048]{1,0:T(8,128)(2,1)S(1)}, u32[]{:S(2)}, u32[]{:S(2)}) collective-permute-start(bf16[64,2048]{1,0:T(8,128)(2,1)S(1)} %pad_maximum_fusion.3), channel_id=1, source_target_pairs={{0,192},{64,0},{128,64},{192,128},{1,193},{65,1},{129,65},{193,129... | collective-permute-start | bytes 786440 | tf_op jit(solution)/shard_map/ppermute | solution.py:205
  144.3 7.6 %collective-permute-start.16 = (bf16[32,2048]{1,0:T(8,128)(2,1)S(1)}, bf16[32,2048]{1,0:T(8,128)(2,1)S(1)}, u32[]{:S(2)}, u32[]{:S(2)}) collective-permute-start(bf16[32,2048]{1,0:T(8,128)(2,1)S(1)} %fusion.6), channel_id=1, source_target_pairs={{0,48},{16,0},{32,16},{48,32},{1,49},{17,1},{33,17},{49,33},{2,50}... | collective-permute-start | bytes 393224 | tf_op jit(solution)/shard_map/ppermute | solution.py:205
  149.4 12.4 %collective-permute-start.24 = (bf16[32,2048]{1,0:T(8,128)(2,1)S(1)}, bf16[32,2048]{1,0:T(8,128)(2,1)S(1)}, u32[]{:S(2)}, u32[]{:S(2)}) collective-permute-start(bf16[32,2048]{1,0:T(8,128)(2,1)S(1)} %fusion), channel_id=1, source_target_pairs={{0,192},{64,0},{128,64},{192,128},{1,193},{65,1},{129,65},{193,129... | collective-permute-start | bytes 393224 | tf_op jit(solution)/shard_map/ppermute | solution.py:205
  152.0 16.4 %collective-permute-start.15 = (bf16[32,2048]{1,0:T(8,128)(2,1)S(1)}, bf16[32,2048]{1,0:T(8,128)(2,1)S(1)}, u32[]{:S(2)}, u32[]{:S(2)}) collective-permute-start(bf16[32,2048]{1,0:T(8,128)(2,1)S(1)} %get-tuple-element.62), channel_id=1, source_target_pairs={{0,16},{16,32},{32,48},{48,0},{1,17},{17,33},{33,49},{49,1},{2,18}... | collective-permute-start | bytes 393224 | tf_op jit(solution)/shard_map/ppermute | solution.py:205
  161.9 6.5 %collective-permute-start.23 = (bf16[32,2048]{1,0:T(8,128)(2,1)S(1)}, bf16[32,2048]{1,0:T(8,128)(2,1)S(1)}, u32[]{:S(2)}, u32[]{:S(2)}) collective-permute-start(bf16[32,2048]{1,0:T(8,128)(2,1)S(1)} %get-tuple-element.60), channel_id=1, source_target_pairs={{0,64},{64,128},{128,192},{192,0},{1,65},{65,129},{129,193},{193,1... | collective-permute-start | bytes 393224 | tf_op jit(solution)/shard_map/ppermute | solution.py:205
  188.8 6.1 %collective-permute-start.25 = (bf16[96,576]{1,0:T(8,128)(2,1)S(1)}, bf16[96,576]{1,0:T(8,128)(2,1)S(1)}, u32[]{:S(2)}, u32[]{:S(2)}) collective-permute-start(bf16[96,576]{1,0:T(8,128)(2,1)S(1)} %get-tuple-element.49), channel_id=1, source_target_pairs={{0,1},{1,2},{2,3},{3,4},{4,5},{5,6},{6,7},{7,0},{8,9},{9,10},{10,1... | collective-permute-start | bytes 331784 | tf_op jit(solution)/shard_map/ppermute | solution.py:205
  188.8 6.2 %collective-permute-start.29 = (bf16[96,576]{1,0:T(8,128)(2,1)S(1)}, bf16[96,576]{1,0:T(8,128)(2,1)S(1)}, u32[]{:S(2)}, u32[]{:S(2)}) collective-permute-start(bf16[96,576]{1,0:T(8,128)(2,1)S(1)} %get-tuple-element.53), channel_id=1, source_target_pairs={{0,7},{1,0},{2,1},{3,2},{4,3},{5,4},{6,5},{7,6},{8,15},{9,8},{10,9... | collective-permute-start | bytes 331784 | tf_op jit(solution)/shard_map/ppermute | solution.py:205
  194.9 7.6 %collective-permute-start.26 = (bf16[192,576]{1,0:T(8,128)(2,1)S(1)}, bf16[192,576]{1,0:T(8,128)(2,1)S(1)}, u32[]{:S(2)}, u32[]{:S(2)}) collective-permute-start(bf16[192,576]{1,0:T(8,128)(2,1)S(1)} %pad_maximum_fusion.6), channel_id=1, source_target_pairs={{0,1},{1,2},{2,3},{3,4},{4,5},{5,6},{6,7},{7,0},{8,9},{9,10},{10,1... | collective-permute-start | bytes 663560 | tf_op jit(solution)/shard_map/ppermute | solution.py:205
  195.1 7.5 %collective-permute-start.30 = (bf16[192,576]{1,0:T(8,128)(2,1)S(1)}, bf16[192,576]{1,0:T(8,128)(2,1)S(1)}, u32[]{:S(2)}, u32[]{:S(2)}) collective-permute-start(bf16[192,576]{1,0:T(8,128)(2,1)S(1)} %pad_maximum_fusion.7), channel_id=1, source_target_pairs={{0,7},{1,0},{2,1},{3,2},{4,3},{5,4},{6,5},{7,6},{8,15},{9,8},{10,9... | collective-permute-start | bytes 663560 | tf_op jit(solution)/shard_map/ppermute | solution.py:205
  202.6 7.5 %collective-permute-start.27 = (bf16[192,576]{1,0:T(8,128)(2,1)S(1)}, bf16[192,576]{1,0:T(8,128)(2,1)S(1)}, u32[]{:S(2)}, u32[]{:S(2)}) collective-permute-start(bf16[192,576]{1,0:T(8,128)(2,1)S(1)} %add_convert_fusion.11), channel_id=1, source_target_pairs={{0,1},{1,2},{2,3},{3,4},{4,5},{5,6},{6,7},{7,0},{8,9},{9,10},{10,1... | collective-permute-start | bytes 663560 | tf_op jit(solution)/shard_map/ppermute | solution.py:205
  202.7 7.5 %collective-permute-start.31 = (bf16[192,576]{1,0:T(8,128)(2,1)S(1)}, bf16[192,576]{1,0:T(8,128)(2,1)S(1)}, u32[]{:S(2)}, u32[]{:S(2)}) collective-permute-start(bf16[192,576]{1,0:T(8,128)(2,1)S(1)} %add_convert_fusion.9), channel_id=1, source_target_pairs={{0,7},{1,0},{2,1},{3,2},{4,3},{5,4},{6,5},{7,6},{8,15},{9,8},{10,9... | collective-permute-start | bytes 663560 | tf_op jit(solution)/shard_map/ppermute | solution.py:205
  210.1 7.5 %collective-permute-start.28 = (bf16[192,576]{1,0:T(8,128)(2,1)S(1)}, bf16[192,576]{1,0:T(8,128)(2,1)S(1)}, u32[]{:S(2)}, u32[]{:S(2)}) collective-permute-start(bf16[192,576]{1,0:T(8,128)(2,1)S(1)} %add_convert_fusion.10), channel_id=1, source_target_pairs={{0,1},{1,2},{2,3},{3,4},{4,5},{5,6},{6,7},{7,0},{8,9},{9,10},{10,1... | collective-permute-start | bytes 663560 | tf_op jit(solution)/shard_map/ppermute | solution.py:205
  210.3 7.3 %collective-permute-start.32 = (bf16[192,576]{1,0:T(8,128)(2,1)S(1)}, bf16[192,576]{1,0:T(8,128)(2,1)S(1)}, u32[]{:S(2)}, u32[]{:S(2)}) collective-permute-start(bf16[192,576]{1,0:T(8,128)(2,1)S(1)} %add_convert_fusion.8), channel_id=1, source_target_pairs={{0,7},{1,0},{2,1},{3,2},{4,3},{5,4},{6,5},{7,6},{8,15},{9,8},{10,9... | collective-permute-start | bytes 663560 | tf_op jit(solution)/shard_map/ppermute | solution.py:205
  219.1 124.1 %all-to-all-start.2 = ((bf16[32,16,576]{2,1,0:T(8,128)(2,1)}), bf16[32,16,576]{2,1,0:T(8,128)(2,1)S(1)}, u32[]{:S(2)}, u32[]{:S(2)}) async-start(bf16[32,16,576]{2,1,0:T(8,128)(2,1)} %shard_map.127), calls=%async_computation.2 | async-start | bytes 1310720 | tf_op jit(solution)/shard_map/all_to_all | solution.py:584
  228.3 113.2 %all-reduce.2.cloned.1.call-start = ((), (), s32[]{:S(2)}) async-start(), calls=%async_computation.3 | async-start | bytes 262144 | tf_op jit(solution)/shard_map/psum | solution.py:556
Sparse Core Ops, SparseCore 0:
  233.0 108.5 all-reduce.1

commit v2 on v1

v2 whole, which is shorter than its diff:
```python
import functools

import jax
import jax.numpy as jnp
from jax import lax
from jax.experimental import pallas as pl
from jax.experimental.pallas import tpu as pltpu
from jax.sharding import Mesh, PartitionSpec as P

SCORE_SCALE = 192.0 ** (-0.5)
ADAPTER_SCALE = 2.0
EXP2_SCALE = SCORE_SCALE * 1.4426950408889634

NX = 4
NY = 4
NCORE = 2
NCTX = 32
NTP = 8
GROUPS = 2
GSLOTS = 6
SLOTS = 12
BLOCK = 128
WIDTH = 576
LATENT = 512
VALUE = 128
HEADS_DEV = 16
QRY_DEV = 128
GQ = 64
RANK = 32
FEATS = 224
HEAD_IN = 2048
HALF_IN = 1024
CHIP_QRY = 256
PIECE = BLOCK // NTP
INFO_LANES = 640
SLOT_LANES = 768
DOWN_AT = 640
PREP_PAIRS = 4
HEAD_CUTS = 2
RING_COLS = 4
CORNER_FLOPS = 1e7
PICK_FLOPS = 1e11
SERVE_FLOPS = 1e6
GROUP_ROWS = GSLOTS * BLOCK
MASKED = -1e30

bf16 = jnp.bfloat16
f32 = jnp.float32

NN = (((1,), (0,)), ((), ()))
NT = (((1,), (1,)), ((), ()))
TN = (((0,), (0,)), ((), ()))


def mm(a, b, dims):
    return lax.dot_general(a, b, dims, preferred_element_type=f32)


def params(mib):
    return pltpu.CompilerParams(vmem_limit_bytes=mib * 1024 * 1024)


def cost(flops, nbytes):
    return pl.CostEstimate(flops=int(flops), bytes_accessed=int(nbytes), transcendentals=0)


def smem():
    return pl.BlockSpec(memory_space=pltpu.SMEM)


def vmem():
    return pl.BlockSpec(memory_space=pltpu.VMEM)


def prep_kernel(
    place,
    ids,
    g_ref,
    up_ref,
    w_ref,
    down_ref,
    saved_ref,
    cache_ref,
    rows_out,
    info,
    w_mine,
    w_other,
    cache_out,
    wcat,
    rows_t,
    block,
):
    step = pl.program_id(0)
    core = place[2]

    @pl.when(step == 0)
    def _():
        wcat[:FEATS, :] = w_ref[...]
        wcat[FEATS:, :] = (ADAPTER_SCALE * down_ref[...].astype(f32)).astype(bf16)
        w_mine[...] = wcat[:, pl.ds(pl.multiple_of(core * HALF_IN, HALF_IN), HALF_IN)]
        w_other[...] = wcat[:, pl.ds(pl.multiple_of((1 - core) * HALF_IN, HALF_IN), HALF_IN)]
        rows_t[...] = mm(down_ref[...], saved_ref[...], NT).astype(bf16)

    rows = rows_t[...]
    start = pl.multiple_of(place[3] * PIECE, PIECE)
    for pair in range(PREP_PAIRS):
        block[pair] = cache_ref[pair].T
        cache_out[pair] = block[pair, pl.ds(start, PIECE), :]
        g = g_ref[:, pair * 2 * QRY_DEV : (pair + 1) * 2 * QRY_DEV]
        low = mm(up_ref[...], g, NN).astype(bf16)
        rows_out[pair] = jnp.concatenate([g, low], axis=0).T
        for half in range(2):
            cols = slice(half * QRY_DEV, (half + 1) * QRY_DEV)
            at = 2 * pair + half
            info[at, :, 0:128] = low[:16, cols]
            info[at, :, 128:256] = low[16:, cols]
            info[at, :, 256:384] = rows[:16]
            info[at, :, 384:512] = rows[16:]
            number = ids[2 * PREP_PAIRS * step + at].astype(f32)
            info[at, :, 512:640] = jnp.full((16, 128), number, f32).astype(bf16)


def prep(place, ids, g_t, up, w_t, down, saved, cache_t):
    pairs = NX * NY
    blocks = cache_t.shape[0]
    step_blocks = blocks * PREP_PAIRS // pairs
    fixed = lambda s, p, i: (0, 0)
    moving = lambda s, p, i: (s, 0, 0)
    return pl.pallas_call(
        prep_kernel,
        grid_spec=pltpu.PrefetchScalarGridSpec(
            num_scalar_prefetch=2,
            grid=(pairs // PREP_PAIRS,),
            in_specs=[
                pl.BlockSpec((FEATS, PREP_PAIRS * 2 * QRY_DEV), lambda s, p, i: (0, s)),
                pl.BlockSpec((RANK, FEATS), fixed),
                pl.BlockSpec((FEATS, HEAD_IN), fixed),
                pl.BlockSpec((RANK, HEAD_IN), fixed),
                pl.BlockSpec((QRY_DEV, HEAD_IN), fixed),
                pl.BlockSpec((step_blocks, WIDTH, BLOCK), moving),
            ],
            out_specs=[
                pl.BlockSpec((PREP_PAIRS, 256, 256), moving),
                pl.BlockSpec((2 * PREP_PAIRS, 16, INFO_LANES), moving),
                pl.BlockSpec((256, HALF_IN), fixed),
                pl.BlockSpec((256, HALF_IN), fixed),
                pl.BlockSpec((step_blocks, PIECE, WIDTH), moving),
            ],
            scratch_shapes=[
                pltpu.VMEM((256, HEAD_IN), bf16),
                pltpu.VMEM((RANK, QRY_DEV), bf16),
                pltpu.VMEM((step_blocks, BLOCK, WIDTH), bf16),
            ],
        ),
        out_shape=[
            jax.ShapeDtypeStruct((pairs, 256, 256), bf16),
            jax.ShapeDtypeStruct((NCTX, 16, INFO_LANES), bf16),
            jax.ShapeDtypeStruct((256, HALF_IN), bf16),
            jax.ShapeDtypeStruct((256, HALF_IN), bf16),
            jax.ShapeDtypeStruct((blocks, PIECE, WIDTH), bf16),
        ],
        compiler_params=params(60),
        cost_estimate=cost(1e8, 6e6),
    )(place, ids, g_t, up, w_t, down, saved, cache_t)


def head_kernel(place, *refs):
    mine, theirs = refs[0:4], refs[4:8]
    w_own, w_pair = refs[8:10]
    (own, p1, m1, p2, m2, mark) = refs[10:]
    step = pl.program_id(0)
    rows = jnp.concatenate(
        [jnp.concatenate([m[0], t[0]], axis=1) for m, t in zip(mine, theirs)], axis=0
    )
    mark[...] = jnp.zeros_like(mark)
    steps = [
        [(own, 0), (own, 1), (own, 2), (own, 3)],
        [(p2, 0), (p2, 1), (p1, 0), (p1, 1)],
        [(p1, 0), (p1, 1), (m1, 0), (m1, 1)],
        [(m1, 0), (m1, 1), (m2, 0), (m2, 1)],
    ]
    for d1, places in enumerate(steps):

        @pl.when(step == d1)
        def _(places=places):
            for cut in range(HEAD_CUTS):
                size = HALF_IN // HEAD_CUTS
                cols = slice(cut * size, (cut + 1) * size)
                w = jnp.concatenate([w_own[:, cols], w_pair[:, cols]], axis=0)
                both = mm(rows, w, NN).astype(bf16)
                for d2, (ref, at) in enumerate(places):
                    ref[at, :, cols] = both[CHIP_QRY * d2 : CHIP_QRY * (d2 + 1)]


def head_partials(place, mine, theirs, w_own, w_pair):
    def row(d2):
        def index(s, p):
            on_x = jnp.where(p[2] == 0, s, d2)
            on_y = jnp.where(p[2] == 0, d2, s)
            return (lax.rem(p[0] + on_x, NX) * NY + lax.rem(p[1] + on_y, NY), 0, 0)

        return pl.BlockSpec((1, CHIP_QRY, 256), index)

    def whole():
        return pl.BlockSpec((256, HALF_IN), lambda s, p: (0, 0))

    def past(s, bound):
        return (s > bound).astype(jnp.int32)

    def out(count, block, index):
        return (
            pl.BlockSpec((block, CHIP_QRY, HALF_IN), lambda s, p: (index(s), 0, 0)),
            jax.ShapeDtypeStruct((count, CHIP_QRY, HALF_IN), bf16),
        )

    outs = [
        out(4, 4, lambda s: 0),
        out(4, 2, lambda s: past(s, 1)),
        out(4, 2, lambda s: past(s, 2)),
        out(2, 2, lambda s: 0),
        out(2, 2, lambda s: 0),
        (
            pl.BlockSpec((8, 128), lambda s, p: (0, 0)),
            jax.ShapeDtypeStruct((8, 128), f32),
        ),
    ]
    return pl.pallas_call(
        head_kernel,
        grid_spec=pltpu.PrefetchScalarGridSpec(
            num_scalar_prefetch=1,
            grid=(4,),
            in_specs=[row(i) for i in range(4)] * 2 + [whole(), whole()],
            out_specs=[o[0] for o in outs],
        ),
        out_shape=[o[1] for o in outs],
        compiler_params=params(60),
        cost_estimate=cost(4.3e9, 13e6),
    )(place, *[mine] * 4, *[theirs] * 4, w_own, w_pair)


def ring(value, order, by):
    pairs = []
    for x in range(NX):
        for y in range(NY):
            for core in range(NCORE):
                if core == order:
                    to = ((x + by) % NX, y)
                else:
                    to = (x, (y + by) % NY)
                pairs.append(((x * NY + y) * 2 + core, (to[0] * NY + to[1]) * 2 + core))
    return lax.ppermute(value, ("x", "y", "core"), pairs)


def shift(value, axis, size, by):
    return lax.ppermute(value, axis, [(i, (i + by) % size) for i in range(size)])


def add(*terms):
    total = terms[0].astype(f32)
    for t in terms[1:]:
        total = total + t.astype(f32)
    return total.astype(bf16)


def call_whole(kernel, outs, mib, flops, nbytes, *args):
    return pl.pallas_call(
        kernel,
        in_specs=[vmem()] * len(args),
        out_specs=[vmem()] * len(outs),
        out_shape=[jax.ShapeDtypeStruct(o, bf16) for o in outs],
        compiler_params=params(mib),
        cost_estimate=cost(flops, nbytes),
    )(*args)


def relay_kernel(p, m, minus, plus, mark, o1, o2):
    o1[...] = add(p[...], minus[...])
    o2[...] = add(m[...], plus[...])


def columns(count, rest, at=0):
    block = (count,) + rest + (HALF_IN // RING_COLS,)
    if rest:
        return pl.BlockSpec(block, lambda s: (at, 0, s))
    return pl.BlockSpec(block, lambda s: (0, s))


def relay(*args):
    return pl.pallas_call(
        relay_kernel,
        grid=(RING_COLS,),
        in_specs=[columns(2, (CHIP_QRY,), at) for at in (0, 0, 1, 0)]
        + [pl.BlockSpec((16, 128), lambda s: (0, 0))],
        out_specs=[columns(2, (CHIP_QRY,))] * 2,
        out_shape=[jax.ShapeDtypeStruct((2, CHIP_QRY, HALF_IN), bf16)] * 2,
        compiler_params=params(60),
        cost_estimate=cost(1e7, 6e6),
    )(*args)


def corner_kernel(own, minus, plus, last_minus, last_plus, mark_a, mark_b, *outs):
    for i in range(2):
        outs[i][...] = add(own[i], plus[i], last_minus[i])
        outs[2 + i][...] = add(own[2 + i], minus[i], last_plus[i])


def corner(*args):
    two = columns(2, (CHIP_QRY,))
    return pl.pallas_call(
        corner_kernel,
        grid=(RING_COLS,),
        in_specs=[columns(4, (CHIP_QRY,)), two, columns(2, (CHIP_QRY,), 1), two, two]
        + [pl.BlockSpec((16, 128), lambda s: (0, 0))] * 2,
        out_specs=[columns(CHIP_QRY, ())] * 4,
        out_shape=[jax.ShapeDtypeStruct((CHIP_QRY, HALF_IN), bf16)] * 4,
        compiler_params=params(60),
        cost_estimate=cost(1e7, 8e6),
    )(*args)


def total_kernel(place, a, b, c, d, mine, other):
    core = place[2]
    here = pl.ds(pl.multiple_of(core * QRY_DEV, QRY_DEV), QRY_DEV)
    there = pl.ds(pl.multiple_of((1 - core) * QRY_DEV, QRY_DEV), QRY_DEV)
    mine[...] = add(a[here, :], b[here, :], c[here, :], d[here, :])
    other[...] = add(a[there, :], b[there, :], c[there, :], d[there, :])


def total(place, *args):
    return pl.pallas_call(
        total_kernel,
        in_specs=[smem()] + [vmem()] * 4,
        out_specs=[vmem()] * 2,
        out_shape=[jax.ShapeDtypeStruct((QRY_DEV, HALF_IN), bf16)] * 2,
        compiler_params=params(60),
        cost_estimate=cost(1e6, 3e6),
    )(place, *args)


def pick_kernel(chosen, got, up_ref, piece, down_out):
    for k in range(SLOTS):
        piece[k * PIECE : (k + 1) * PIECE, :] = got[chosen[k], :, :WIDTH]
    base = SLOTS * PIECE
    piece[base : base + 16, :] = jnp.zeros((16, WIDTH), bf16)
    piece[base : base + 16, :FEATS] = up_ref[:16]
    piece[base : base + 16, 256 : 256 + FEATS] = up_ref[16:]
    down = got[0, :, DOWN_AT:].astype(f32)
    for s in range(1, NCTX):
        down = down + got[s, :, DOWN_AT:].astype(f32)
    down_out[...] = down.astype(bf16)


def pick(chosen, got, up):
    outs = [(SLOTS * PIECE + 16, WIDTH), (16, 128)]
    return pl.pallas_call(
        pick_kernel,
        in_specs=[smem(), vmem(), vmem()],
        out_specs=[vmem()] * 2,
        out_shape=[jax.ShapeDtypeStruct(o, bf16) for o in outs],
        compiler_params=params(60),
        cost_estimate=cost(PICK_FLOPS, 1e6),
    )(chosen, got, up)


def serve_kernel(ids, cache_ref, info, saved_ref, mark, out_ref):
    low0 = info[0, :, 0:128].astype(f32)
    low1 = info[0, :, 128:256].astype(f32)
    for s in range(1, NCTX):
        low0 = low0 + info[s, :, 0:128].astype(f32)
        low1 = low1 + info[s, :, 128:256].astype(f32)
    low = (ADAPTER_SCALE * jnp.concatenate([low0, low1], axis=0)).astype(bf16)
    down = mm(low, saved_ref[...], NN).astype(bf16)
    for s in range(NCTX):
        row, col = 16 * (s // 16), 128 * (s % 16)
        out_ref[s, :, :WIDTH] = cache_ref[ids[s]]
        out_ref[s, :, DOWN_AT:] = down[row : row + 16, col : col + 128]


def serve(ids, cache_piece, info, saved, mark):
    return pl.pallas_call(
        serve_kernel,
        in_specs=[smem()] + [vmem()] * 4,
        out_specs=vmem(),
        out_shape=jax.ShapeDtypeStruct((NCTX, PIECE, SLOT_LANES), bf16),
        compiler_params=params(60),
        cost_estimate=cost(SERVE_FLOPS, 2e6),
    )(ids, cache_piece, info, saved, mark)


def up_kernel(info, g_ref, mark, up_out, rows_all):
    for s in range(NCTX):
        rows_all[0:16, s * 128 : (s + 1) * 128] = info[s, :, 256:384]
        rows_all[16:32, s * 128 : (s + 1) * 128] = info[s, :, 384:512]
    up_out[...] = mm(rows_all[...], g_ref[...], NT).astype(bf16)


def up_partial(info, g_t, mark):
    return pl.pallas_call(
        up_kernel,
        in_specs=[vmem()] * 3,
        out_specs=vmem(),
        out_shape=jax.ShapeDtypeStruct((RANK, FEATS), bf16),
        scratch_shapes=[pltpu.VMEM((RANK, NCTX * QRY_DEV), bf16)],
        compiler_params=params(60),
        cost_estimate=cost(1e8, 3e6),
    )(info, g_t, mark)


def gather_tp(own):
    pieces = [None] * NTP
    pieces[0] = own
    forward = own
    back = own
    for step in range(1, 5):
        forward = shift(forward, "tp", NTP, -1)
        pieces[step] = forward
        if step < 4:
            back = shift(back, "tp", NTP, 1)
            pieces[NTP - step] = back
    return pieces


def attend_kernel(place, *refs):
    pieces = refs[:NTP]
    q_ref, vu_ref, bias_ref, hg_mine, hg_other = refs[NTP : NTP + 5]
    dq_ref, up_ref = refs[NTP + 5 : NTP + 7]
    outs = refs[NTP + 7 : NTP + 16]
    keys, keys_t, spread, ds_all, p_all, q_all, og_all = refs[NTP + 16 :]
    step = pl.program_id(0)
    span = GSLOTS * PIECE
    lanes = 4 * GQ

    @pl.when(step == 0)
    def _():
        for d in range(NTP):
            for g in range(GROUPS):
                keys[g, d * span : (d + 1) * span, :] = pieces[d][g * span : (g + 1) * span, :]
        for g in range(GROUPS):
            keys_t[g] = keys[g].T
        spread[...] = jnp.zeros_like(spread)
        base = SLOTS * PIECE
        total = pieces[0][base : base + 16, :512].astype(f32)
        for d in range(1, NTP):
            total = total + pieces[d][base : base + 16, :512].astype(f32)
        up_ref[:16, :] = ADAPTER_SCALE * total[:, :FEATS]
        up_ref[16:, :] = ADAPTER_SCALE * total[:, 256 : 256 + FEATS]

    here = pl.ds(pl.multiple_of(step * lanes, lanes), lanes)
    hg = jnp.where(step // 2 == place[2], hg_mine[...], hg_other[...])
    maps = jnp.concatenate([vu_ref[h] for h in range(4)], axis=1)
    dqs = []
    for g in range(GROUPS):
        q4 = jnp.concatenate([q_ref[h][:, g * GQ : (g + 1) * GQ] for h in range(4)], axis=1)
        for h in range(4):
            cols = slice(h * VALUE, (h + 1) * VALUE)
            spread[g, h * GQ : (h + 1) * GQ, cols] = hg[g * GQ : (g + 1) * GQ, cols]
        og = mm(maps, spread[g], NT).astype(bf16)
        q_all[g, :, here] = q4
        og_all[g, :, here] = og
        s = mm(keys[g], q4, NN)
        s = s.reshape(NTP, GSLOTS, PIECE, lanes) * EXP2_SCALE + bias_ref[g][None, :, None, :]
        s = s.reshape(GROUP_ROWS, lanes)
        e = jnp.exp2(s - jnp.max(s, axis=0, keepdims=True))
        share = 1.0 / jnp.sum(e, axis=0, keepdims=True)
        dp = mm(keys[g, :, :LATENT], og, NN)
        delta = jnp.sum(e * dp, axis=0, keepdims=True) * share
        ds = (e * ((dp - delta) * (share * SCORE_SCALE))).astype(bf16)
        p_all[g, :, here] = (e * share).astype(bf16)
        ds_all[g, :, here] = ds
        dqs.append(mm(keys_t[g], ds, NN).astype(bf16))
    for h in range(4):
        cols = slice(h * GQ, (h + 1) * GQ)
        dq_ref[h] = jnp.concatenate([dqs[0][:, cols], dqs[1][:, cols]], axis=1)

    @pl.when(step == pl.num_programs(0) - 1)
    def _():
        for g in range(GROUPS):
            grads = mm(ds_all[g], q_all[g], NT)
            latent = grads[:, :LATENT] + mm(p_all[g], og_all[g], NT)
            latent = latent.astype(bf16)
            rope = grads[:, LATENT:].astype(bf16)
            for d in range(NTP):
                ref = outs[d] if d < 4 else (outs[4 + g] if d == 4 else outs[d + 1])
                at = 0 if d == 4 else g * span
                ref[at : at + span, :LATENT] = latent[d * span : (d + 1) * span]
                ref[at : at + span, LATENT:] = rope[d * span : (d + 1) * span]


def attend(place, pieces, q_t, vu, bias, hg_mine, hg_other):
    span = GSLOTS * PIECE
    whole = lambda s: (0, 0)
    rows = [2 * span] * 4 + [span] * 2 + [2 * span] * 3
    out_specs = [
        pl.BlockSpec((4, WIDTH, QRY_DEV), lambda s: (s, 0, 0)),
        pl.BlockSpec((RANK, FEATS), whole),
    ]
    out_specs += [pl.BlockSpec((n, WIDTH), whole) for n in rows]
    out_shape = [
        jax.ShapeDtypeStruct((HEADS_DEV, WIDTH, QRY_DEV), bf16),
        jax.ShapeDtypeStruct((RANK, FEATS), f32),
    ]
    out_shape += [jax.ShapeDtypeStruct((n, WIDTH), bf16) for n in rows]
    hg_spec = pl.BlockSpec((QRY_DEV, 4 * VALUE), lambda s: (0, lax.rem(s, 2)))
    width = HEADS_DEV * GQ
    return pl.pallas_call(
        attend_kernel,
        grid=(HEADS_DEV // 4,),
        in_specs=[smem()]
        + [pl.BlockSpec(pieces[0].shape, whole)] * NTP
        + [
            pl.BlockSpec((4, WIDTH, QRY_DEV), lambda s: (s, 0, 0)),
            pl.BlockSpec((4, LATENT, VALUE), lambda s: (s, 0, 0)),
            pl.BlockSpec(bias.shape, lambda s: (0, 0, 0)),
        ]
        + [hg_spec] * 2,
        out_specs=out_specs,
        out_shape=out_shape,
        scratch_shapes=[
            pltpu.VMEM((GROUPS, GROUP_ROWS, WIDTH), bf16),
            pltpu.VMEM((GROUPS, WIDTH, GROUP_ROWS), bf16),
            pltpu.VMEM((GROUPS, 4 * GQ, 4 * VALUE), bf16),
            pltpu.VMEM((GROUPS, GROUP_ROWS, width), bf16),
            pltpu.VMEM((GROUPS, GROUP_ROWS, width), bf16),
            pltpu.VMEM((GROUPS, WIDTH, width), bf16),
            pltpu.VMEM((GROUPS, LATENT, width), bf16),
        ],
        compiler_params=params(60),
        cost_estimate=cost(1e10, 1.2e7),
    )(place, *pieces, q_t, vu, bias, hg_mine, hg_other)


def reduce_tp(parts):
    d0, d1, d2, d3, d4a, d4b, d5, d6, d7 = parts
    half = d4a.shape[0]
    up = shift(d4a, "tp", NTP, 1)
    down = shift(d4b, "tp", NTP, -1)
    up = shift(jnp.concatenate([add(d3[:half], up), d3[half:]], axis=0), "tp", NTP, 1)
    down = shift(jnp.concatenate([d5[:half], add(d5[half:], down)], axis=0), "tp", NTP, -1)
    up = shift(add(d2, up), "tp", NTP, 1)
    down = shift(add(d6, down), "tp", NTP, -1)
    up = shift(add(d1, up), "tp", NTP, 1)
    down = shift(add(d7, down), "tp", NTP, -1)
    return d0, up, down


def slots_kernel(chosen, own, up, down, sums, out_ref):
    total = own[...].astype(f32) + up[...].astype(f32) + down[...].astype(f32)
    total = total.astype(bf16)
    empty = jnp.zeros((PIECE, WIDTH), bf16)
    for s in range(NCTX):
        out_ref[s, :, :WIDTH] = empty
        out_ref[s, :, DOWN_AT:] = sums[...]
    for k in range(SLOTS):
        out_ref[chosen[k], :, :WIDTH] = total[k * PIECE : (k + 1) * PIECE, :]


def to_slots(chosen, own, up, down, sums):
    return pl.pallas_call(
        slots_kernel,
        in_specs=[smem()] + [vmem()] * 4,
        out_specs=vmem(),
        out_shape=jax.ShapeDtypeStruct((NCTX, PIECE, SLOT_LANES), bf16),
        compiler_params=params(60),
        cost_estimate=cost(1e6, 2e6),
    )(chosen, own, up, down, sums)


def collect_kernel(ids, got_ref, out_ref, down_ref):
    out_ref[...] = jnp.zeros_like(out_ref)
    for s in range(NCTX):
        row, col = 16 * (s // 16), 128 * (s % 16)
        down_ref[row : row + 16, col : col + 128] = got_ref[s, :, DOWN_AT:].astype(f32)
        out_ref[ids[s]] += got_ref[s, :, :WIDTH].astype(f32)


def collect(ids, got, blocks):
    return pl.pallas_call(
        collect_kernel,
        in_specs=[smem(), vmem()],
        out_specs=[vmem(), vmem()],
        out_shape=[
            jax.ShapeDtypeStruct((blocks, PIECE, WIDTH), f32),
            jax.ShapeDtypeStruct((RANK, HEAD_IN), f32),
        ],
        compiler_params=params(60),
        cost_estimate=cost(1e6, 2e6),
    )(ids, got)


def shards(
    queries,
    latent_block_cache,
    selected_block_lists,
    output_gradient,
    output_weight,
    adapter_down,
    adapter_up,
    value_up_map,
    saved_head_input,
):
    ctx_axes = ("x", "y", "core")
    blocks_dev = latent_block_cache.shape[0]
    place = jnp.stack(
        [lax.axis_index("x"), lax.axis_index("y"), lax.axis_index("core"), lax.axis_index("tp")]
    ).astype(jnp.int32)

    holder = selected_block_lists // blocks_dev
    local = selected_block_lists - holder * blocks_dev
    every = jnp.arange(NCTX, dtype=jnp.int32)
    hit = holder[:, :, None] == every[None, None, :]
    wanted = jnp.max(jnp.where(hit, local[:, :, None], 0), axis=(0, 1))
    g_t = output_gradient.T
    mine, info, w_own, w_other, cache_piece = prep(
        place,
        wanted,
        g_t,
        adapter_up,
        output_weight.T,
        adapter_down,
        saved_head_input,
        jnp.swapaxes(latent_block_cache, 1, 2),
    )
    theirs = shift(mine, "core", 2, 1)
    w_pair = shift(w_other, "core", 2, 1)
    info = lax.all_to_all(info, ctx_axes, split_axis=0, concat_axis=0, tiled=True)

    used = jnp.any(hit.reshape(GROUPS, GQ * hit.shape[1], NCTX), axis=1).astype(jnp.int32)
    rank = jnp.cumsum(used, axis=1)
    slot_hit = (used[:, None, :] == 1) & (
        rank[:, None, :] == jnp.arange(1, GSLOTS + 1, dtype=jnp.int32)[None, :, None]
    )
    chosen = jnp.sum(jnp.where(slot_hit, every[None, None, :], 0), axis=2).reshape(SLOTS)
    holder_groups = holder.reshape(GROUPS, GQ, holder.shape[1])
    picked = jnp.any(
        holder_groups[:, None, :, :] == chosen.reshape(GROUPS, GSLOTS)[:, :, None, None], axis=3
    )
    bias = jnp.where(picked, 0.0, MASKED).astype(f32)
    bias = jnp.concatenate([bias] * 4, axis=2)

    own, p1, m1, p2, m2, mark = head_partials(place, mine, theirs, w_own, w_pair)
    ids = (info[:, 0, 512].astype(f32) + mark[0, 0]).astype(jnp.int32)
    minus = ring(p1, 0, 1)
    plus = ring(m1, 0, -1)

    slots = serve(ids, cache_piece, info, saved_head_input, mark)
    got = lax.all_to_all(slots, ctx_axes, split_axis=0, concat_axis=0, tiled=True)
    up_part = up_partial(info, g_t, mark)
    piece, down_sums = pick(chosen, got, up_part)
    pieces = gather_tp(piece)
    p2, m2 = relay(p2, m2, minus, plus, pieces[1])
    last_minus = ring(p2, 0, 1)
    last_plus = ring(m2, 0, -1)
    sums = corner(own, minus, plus, last_minus, last_plus, pieces[3], pieces[6])
    hg_mine, hg_other = total(place, sums[0], *[ring(sums[i], 1, i) for i in (1, 2, 3)])
    hg_other = shift(hg_other, "core", 2, 1)

    dq_t, up_gradient, *parts = attend(
        place,
        pieces,
        jnp.transpose(queries, (1, 2, 0)),
        value_up_map,
        bias,
        hg_mine,
        hg_other,
    )
    query_grads = jnp.transpose(dq_t, (2, 0, 1))

    own, up, down = reduce_tp(parts)
    slots = to_slots(chosen, own, up, down, down_sums)
    returned = lax.all_to_all(slots, ctx_axes, split_axis=0, concat_axis=0, tiled=True)
    cache_grads, down_gradient = collect(ids, returned, blocks_dev)
    return (query_grads, cache_grads, down_gradient, up_gradient)


def solution(mesh):
    split = Mesh(mesh.devices.reshape(NX, NY, NCORE, NTP), ("x", "y", "core", "tp"))
    ctx = ("x", "y", "core")
    placed = (
        P(ctx, "tp", None),
        P(ctx, None, None),
        P(ctx, None),
        P(None, ctx),
        P("tp", ctx),
        P(None, "tp"),
        P(None, ctx),
        P("tp", None, None),
        P(ctx, "tp"),
    )
    return jax.shard_map(
        shards,
        mesh=split,
        in_specs=placed,
        out_specs=(P(ctx, "tp", None), P(ctx, "tp", None), P(None, "tp"), P(None, ctx)),
        check_vma=False,
    )
```

time: 358 us -> 221 us (0.62)
  waiting for transfers between devices: 171 us -> 59.7 us
  starting transfers between devices: 88.4 us -> 55.9 us
  blocking collectives: 0 us -> 18.7 us
  between operations: 14.7 us -> 0.96 us
  Pallas kernels: 49.6 us -> 63 us
  local copies, waits for them, and re-layouts: 17.8 us -> 11.5 us
    psum x1 -> x0, waiting for transfers between devices: 112 us -> none  [shards(): down_gradient = lax.psum(down_part, ctx_axes).astype(f32)]
    ppermute x33 -> x18, starting transfers between devices: 66.5 us -> 33.6 us  [shift(): lax.ppermute(value, axis, [(i, (i + by) % size) for i in range(size)])]
    all_to_all x0 -> x1, blocking collectives: none -> 18.7 us  [shards(): lax.all_to_all(slots, ctx_axes, split_axis=0, concat_axis=0, tiled=True)]
    ppermute x33 -> x18, waiting for transfers between devices: 55.3 us -> 37.8 us  [shift(): lax.ppermute(value, axis, [(i, (i + by) % size) for i in range(size)])]
    ppermute x0 -> x7, waiting for transfers between devices: none -> 16.3 us  [ring(): return lax.ppermute(value, ('x', 'y', 'core'), pairs)]
    pallas_call x7 -> x8, Pallas kernels: 28.1 us -> 43 us  [the longest x1 21.6 us: attend(): pl.pallas_call(attend_kernel, grid=(HEADS_DEV // 4,), in_specs=[smem()] +...]
    unnamed x52 -> x50, local copies, waits for them, and re-layouts: 15.9 us -> 7.4 us
    ppermute x0 -> x7, starting transfers between devices: none -> 7.36 us  [ring(): return lax.ppermute(value, ('x', 'y', 'core'), pairs)]
  transfers between devices with their start and end apart: 37 -> 27, of which waited for: 17 -> 15; matrix products, arithmetic and copies ran while one was open for 3% -> 4% of each run, Pallas kernels for 5% -> 9%
where the time goes in v2:
time: 221 us; the launch traced here: 217 us
  Pallas kernels  63 us (29%)
  waiting for transfers between devices  59.7 us (27%)
  starting transfers between devices  55.9 us (25%)
  blocking collectives  18.7 us (8%)
  local copies, waits for them, and re-layouts  11.5 us (5%)
  other arithmetic  7.48 us (3%)
    ppermute x18, waiting for transfers between devices, shift(): lax.ppermute(value, axis, [(i, (i + by) % size) for i in range(size)])  37.8 us
    ppermute x18, starting transfers between devices, shift(): lax.ppermute(value, axis, [(i, (i + by) % size) for i in range(size)])  33.6 us
    pallas_call x1, Pallas kernels, attend(): pl.pallas_call(attend_kernel, grid=(HEADS_DEV // 4,), in_specs=[smem()] +...  21.6 us
    all_to_all x1, blocking collectives, shards(): lax.all_to_all(slots, ctx_axes, split_axis=0, concat_axis=0, tiled=True)  18.7 us
    ppermute x7, waiting for transfers between devices, ring(): return lax.ppermute(value, ('x', 'y', 'core'), pairs)  16.3 us
    pallas_call x1, Pallas kernels, head_partials(): pl.pallas_call(head_kernel, grid_spec=pltpu.PrefetchScalarGridSpec(num_sc...  11.2 us
    all_to_all x1, starting transfers between devices, shards(): lax.all_to_all(info, ctx_axes, split_axis=0, concat_axis=0, tiled=True)  7.62 us
    unnamed x50, local copies, waits for them, and re-layouts  7.4 us
  transfers between devices with their start and end apart: 27, of which 15 were waited for; matrix products, arithmetic and copies ran while one was open for 4% of the time, Pallas kernels for 9%

profile of v2, /device:TPU:2, one launch (start us, length us, event | category | flops | bytes accessed | tf_op | source)
XLA Modules:
  0.0 217.2 jit_solution(16680575144422105061)
XLA Ops:
  0.6 0.7 multiply_subtract_fusion
  1.3 0.7 select_reduce_fusion.ids
  2.0 0.7 pad_add_fusion.place
  2.7 6.9 %shard_map.120 = (bf16[16,256,256]{2,1,0:T(8,128)(2,1)}, bf16[32,16,640]{2,1,0:T(8,128)(2,1)}, bf16[256,1024]{1,0:T(8,128)(2,1)}, bf16[256,1024]{1,0:T(8,128)(2,1)}, bf16[16,16,576]{2,1,0:T(8,128)(2,1)}) custom-call(s32[4]{0:T(128)} %pad_add_fusion.place, s32[32]{0:T(128)} %select_reduce_fusion.ids, bf16[224,4096]{1,0:T(8,128)(2,1)} %bitcast.12, ...), custom_call_target="tpu_custom_call" | custom-call | flops 100000000 | bytes 6000000 | tf_op jit(solution)/shard_map/pallas_call | solution.py:129
  9.7 0.5 collective-permute-start.1
  10.2 7.6 %all-to-all-start = ((bf16[32,16,640]{2,1,0:T(8,128)(2,1)}), bf16[32,16,640]{2,1,0:T(8,128)(2,1)S(1)}, u32[]{:S(2)}, u32[]{:S(2)}) async-start(bf16[32,16,640]{2,1,0:T(8,128)(2,1)} %get-tuple-element.38), calls=%async_computation | async-start | bytes 1310720 | tf_op jit(solution)/shard_map/all_to_all | solution.py:625
  17.9 0.8 copy-done.9
  18.6 0.7 copy-done
  19.3 11.2 %shard_map.121 = (bf16[4,256,1024]{2,1,0:T(8,128)(2,1)}, bf16[4,256,1024]{2,1,0:T(8,128)(2,1)}, bf16[4,256,1024]{2,1,0:T(8,128)(2,1)}, bf16[2,256,1024]{2,1,0:T(...) custom-call(s32[4]{0:T(128)} %pad_add_fusion.place, ...), custom_call_target="tpu_custom_call" | custom-call | flops 4300000256 | bytes 13000000 | tf_op jit(solution)/shard_map/pallas_call | solution.py:227
  30.6 1.2 slice.19
  31.8 1.9 fusion.3.ids
  33.6 2.5 %shard_map.122 = bf16[32,16,768]{2,1,0:T(8,128)(2,1)} custom-call(s32[32]{0:T(128)} %fusion.3.ids, bf16[16,16,576]{2,1,0:T(8,128)(2,1)} %get-tuple-element.43.cache_ref, bf16[32,16,640]{2,1,0:T(8,128)(2,1)} %copy-done.2, bf16[128,2048]{1,0:T(8,128)(2,1)} %saved_ref.3, f32[8,128]{1,0:T(8,128)} %get-tuple-element.42.mark), custom_call_target="tpu_custom_call" | custom-call | flops 1000000 | bytes 2000000 | tf_op jit(solution)/shard_map/pallas_call | solution.py:380
  36.1 7.4 %all-to-all-start.1 = ((bf16[32,16,768]{2,1,0:T(8,128)(2,1)}), bf16[32,16,768]{2,1,0:T(8,128)(2,1)S(1)}, u32[]{:S(2)}, u32[]{:S(2)}) async-start(bf16[32,16,768]{2,1,0:T(8,128)(2,1)} %shard_map.122), calls=%async_computation.1 | async-start | bytes 1572864 | tf_op jit(solution)/shard_map/all_to_all | solution.py:646
  44.4 0.6 reshape.36.chosen
  45.2 1.8 collective-permute-start.9
  47.0 2.9 %shard_map.123.up_ref = bf16[32,224]{1,0:T(8,128)(2,1)} custom-call(bf16[32,16,640]{2,1,0:T(8,128)(2,1)} %copy-done.2, bf16[224,4096]{1,0:T(8,128)(2,1)} %bitcast.13, f32[8,128]{1,0:T(8,128)} %get-tuple-element.42.mark), custom_call_target="tpu_custom_call" | custom-call | flops 100000000 | bytes 3000000 | tf_op jit(solution)/shard_map/pallas_call | solution.py:398
  49.9 5.6 %all-to-all-done.1.got = bf16[32,16,768]{2,1,0:T(8,128)(2,1)S(1)} async-done(((bf16[32,16,768]{2,1,0:T(8,128)(2,1)}), bf16[32,16,768]{2,1,0:T(8,128)(2,1)S(1)}, u32[]{:S(2)}, u32[]{:S(2)}) %all-to-all-start.1) | async-done | bytes 786464 | tf_op jit(solution)/shard_map/all_to_all | solution.py:646
  55.5 0.9 copy-done.5
  56.4 1.9 shard_map.124
  58.3 5.9 %collective-permute-start.2 = (bf16[208,576]{1,0:T(8,128)(2,1)}, bf16[208,576]{1,0:T(8,128)(2,1)S(1)}, u32[]{:S(2)}, u32[]{:S(2)}) collective-permute-start(bf16[208,576]{1,0:T(8,128)(2,1)} %get-tuple-element.44.refs_0_), channel_id=1, source_target_pairs={{0,7},{1,0},{2,1},{3,2},{4,3},{5,4},{6,5},{7,6},{8,15},{9,8},{10,9... | collective-permute-start | bytes 718856 | tf_op jit(solution)/shard_map/ppermute | solution.py:255
  64.2 6.8 %collective-permute-done.2.mark.refs_1_ = bf16[208,576]{1,0:T(8,128)(2,1)S(1)} collective-permute-done((bf16[208,576]{1,0:T(8,128)(2,1)}, bf16[208,576]{1,0:T(8,128)(2,1)S(1)}, u32[]{:S(2)}, u32[]{:S(2)}) %collective-permute-start.2) | collective-permute-done | bytes 239648 | tf_op jit(solution)/shard_map/ppermute | solution.py:255
  71.0 5.9 %collective-permute-done.10.plus = bf16[4,256,1024]{2,1,0:T(8,128)(2,1)S(1)} collective-permute-done((bf16[4,256,1024]{2,1,0:T(8,128)(2,1)}, bf16[4,256,1024]{2,1,0:T(8,128)(2,1)S(1)}, u32[]{:S(2)}, u32[]{:S(2)}) %collective-permute-start.10) | collective-permute-done | bytes 2097184 | tf_op jit(solution)/shard_map/ppermute | solution.py:251
  76.9 1.3 copy-done.1
  78.2 4.3 %shard_map.125 = (bf16[2,256,1024]{2,1,0:T(8,128)(2,1)}, bf16[2,256,1024]{2,1,0:T(8,128)(2,1)}) custom-call(bf16[2,256,1024]{2,1,0:T(8,128)(2,1)} %get-tuple-element.48.p, bf16[2,256,1024]{2,1,0:T(8,128)(2,1)} %get-tuple-element.49.m, bf16[4,256,1024]{2,1,0:T(8,128)(2,1)} %collective-permute-done.9.minus, bf16[4,256,1024]{2,1,0:T(8,128)(2,1)} %copy-done.1, ...), custom_call_target="tpu_custom_call" | custom-call | flops 10000000 | bytes 6000000 | tf_op jit(solution)/shard_map/pallas_call | solution.py:289
  82.6 1.2 collective-permute-start.11
  83.8 0.8 collective-permute-start.12
  84.6 1.9 collective-permute-start.6
  86.5 4.0 %collective-permute-start.3 = (bf16[208,576]{1,0:T(8,128)(2,1)}, bf16[208,576]{1,0:T(8,128)(2,1)S(1)}, u32[]{:S(2)}, u32[]{:S(2)}) collective-permute-start(bf16[208,576]{1,0:T(8,128)(2,1)} %copy-done.12), channel_id=1, source_target_pairs={{0,7},{1,0},{2,1},{3,2},{4,3},{5,4},{6,5},{7,6},{8,15},{9,8},{10,9... | collective-permute-start | bytes 718856 | tf_op jit(solution)/shard_map/ppermute | solution.py:255
  90.5 7.2 %collective-permute-done.6.refs_7_ = bf16[208,576]{1,0:T(8,128)(2,1)S(1)} collective-permute-done((bf16[208,576]{1,0:T(8,128)(2,1)S(1)}, bf16[208,576]{1,0:T(8,128)(2,1)S(1)}, u32[]{:S(2)}, u32[]{:S(2)}) %collective-permute-start.6) | collective-permute-done | bytes 239648 | tf_op jit(solution)/shard_map/ppermute | solution.py:255
  97.7 3.3 %collective-permute-start.4 = (bf16[208,576]{1,0:T(8,128)(2,1)S(1)}, bf16[208,576]{1,0:T(8,128)(2,1)S(1)}, u32[]{:S(2)}, u32[]{:S(2)}) collective-permute-start(bf16[208,576]{1,0:T(8,128)(2,1)S(1)} %collective-permute-done.3.refs_2_), channel_id=1, source_target_pairs={{0,7},{1,0},{2,1},{3,2},{4,3},{5,4},{6,5},{7,6},{8,15},{9,8},{10,9... | collective-permute-start | bytes 718856 | tf_op jit(solution)/shard_map/ppermute | solution.py:255
  101.0 6.3 %collective-permute-done.7.mark_b.refs_6_ = bf16[208,576]{1,0:T(8,128)(2,1)S(1)} collective-permute-done((bf16[208,576]{1,0:T(8,128)(2,1)S(1)}, bf16[208,576]{1,0:T(8,128)(2,1)S(1)}, u32[]{:S(2)}, u32[]{:S(2)}) %collective-permute-start.7) | collective-permute-done | bytes 239648 | tf_op jit(solution)/shard_map/ppermute | solution.py:255
  107.3 0.7 copy-done.10
  108.1 0.3 copy-done.3
  108.5 0.3 copy-done.4
  108.8 4.7 %shard_map.126 = (bf16[256,1024]{1,0:T(8,128)(2,1)}, bf16[256,1024]{1,0:T(8,128)(2,1)}, bf16[256,1024]{1,0:T(8,128)(2,1)}, bf16[256,1024]{1,0:T(8,128)(2,1)}) custom-call(bf16[4,256,1024]{2,1,0:T(8,128)(2,1)} %get-tuple-element.45.own, bf16[4,256,1024]{2,1,0:T(8,128)(2,1)} %collective-permute-done.9.minus, bf16[4,256,1024]{2,1,0:T(8,128)(2,1)} %copy-done.1, ...), custom_call_target="tpu_custom_call" | custom-call | flops 10000000 | bytes 8000000 | tf_op jit(solution)/shard_map/pallas_call | solution.py:309
  113.8 3.0 %collective-permute-start.15 = (bf16[256,1024]{1,0:T(8,128)(2,1)}, bf16[256,1024]{1,0:T(8,128)(2,1)S(1)}, u32[]{:S(2)}, u32[]{:S(2)}) collective-permute-start(bf16[256,1024]{1,0:T(8,128)(2,1)} %get-tuple-element.55), channel_id=1, source_target_pairs={{0,48},{8,200},{16,0},{24,216},{32,16},{40,232},{48,32},{56,248},{... | collective-permute-start | bytes 1572872 | tf_op jit(solution)/shard_map/ppermute | solution.py:251
  117.1 3.2 %collective-permute-start.5 = (bf16[208,576]{1,0:T(8,128)(2,1)}, bf16[208,576]{1,0:T(8,128)(2,1)S(1)}, u32[]{:S(2)}, u32[]{:S(2)}) collective-permute-start(bf16[208,576]{1,0:T(8,128)(2,1)} %copy-done.11), channel_id=1, source_target_pairs={{0,7},{1,0},{2,1},{3,2},{4,3},{5,4},{6,5},{7,6},{8,15},{9,8},{10,9... | collective-permute-start | bytes 718856 | tf_op jit(solution)/shard_map/ppermute | solution.py:255
  120.3 9.5 %collective-permute-done.13.b = bf16[256,1024]{1,0:T(8,128)(2,1)S(1)} collective-permute-done((bf16[256,1024]{1,0:T(8,128)(2,1)}, bf16[256,1024]{1,0:T(8,128)(2,1)S(1)}, u32[]{:S(2)}, u32[]{:S(2)}) %collective-permute-start.13) | collective-permute-done | bytes 524320 | tf_op jit(solution)/shard_map/ppermute | solution.py:251
  129.8 0.9 collective-permute-done.15.d
  130.8 0.8 copy-done.8
  131.6 2.5 %shard_map.127 = (bf16[128,1024]{1,0:T(8,128)(2,1)}, bf16[128,1024]{1,0:T(8,128)(2,1)}) custom-call(s32[4]{0:T(128)} %pad_add_fusion.place, bf16[256,1024]{1,0:T(8,128)(2,1)} %get-tuple-element.52.a, bf16[256,1024]{1,0:T(8,128)(2,1)} %copy-done.6, bf16[256,1024]{1,0:T(8,128)(2,1)} %copy-done.7, bf16[256,1024]{1,0:T(8,128)(2,1)} %copy-done.8), custom_call_target="tpu_custom_call" | custom-call | flops 1000000 | bytes 3000000 | tf_op jit(solution)/shard_map/pallas_call | solution.py:330
  134.1 0.7 pad_maximum_fusion.2.refs_10_
  134.8 1.0 collective-permute-done.16.refs_12_
  135.8 0.7 copy-done.24
  136.5 21.6 %shard_map.128 = (bf16[16,576,128]{2,1,0:T(8,128)(2,1)}, f32[32,224]{1,0:T(8,128)}, bf16[192,576]{1,0:T(8,128)(2,1)}, bf16[192,576]{1,0:T(8,128)(2,1)}, bf16[192...) custom-call(s32[4]{0:T(128)} %pad_add_fusion.place, ...), custom_call_target="tpu_custom_call" | custom-call | flops 10000000000 | bytes 12000000 | tf_op jit(solution)/shard_map/pallas_call | solution.py:505
  158.2 3.1 %collective-permute-start.21 = (bf16[96,576]{1,0:T(8,128)(2,1)}, bf16[96,576]{1,0:T(8,128)(2,1)S(1)}, u32[]{:S(2)}, u32[]{:S(2)}) collective-permute-start(bf16[96,576]{1,0:T(8,128)(2,1)} %get-tuple-element.67), channel_id=1, source_target_pairs={{0,7},{1,0},{2,1},{3,2},{4,3},{5,4},{6,5},{7,6},{8,15},{9,8},{10,9... | collective-permute-start | bytes 331784 | tf_op jit(solution)/shard_map/ppermute | solution.py:255
  161.2 0.9 slice.22
  162.3 0.9 slice.21
  163.2 1.2 collective-permute-done.21
  164.4 0.9 add_convert_fusion.4
  165.4 3.7 %collective-permute-start.22 = (bf16[192,576]{1,0:T(8,128)(2,1)S(1)}, bf16[192,576]{1,0:T(8,128)(2,1)S(1)}, u32[]{:S(2)}, u32[]{:S(2)}) collective-permute-start(bf16[192,576]{1,0:T(8,128)(2,1)S(1)} %pad_maximum_fusion.1), channel_id=1, source_target_pairs={{0,7},{1,0},{2,1},{3,2},{4,3},{5,4},{6,5},{7,6},{8,15},{9,8},{10,9... | collective-permute-start | bytes 663560 | tf_op jit(solution)/shard_map/ppermute | solution.py:255
  169.1 0.9 add_convert_fusion.5
  170.2 3.6 %collective-permute-done.22 = bf16[192,576]{1,0:T(8,128)(2,1)S(1)} collective-permute-done((bf16[192,576]{1,0:T(8,128)(2,1)S(1)}, bf16[192,576]{1,0:T(8,128)(2,1)S(1)}, u32[]{:S(2)}, u32[]{:S(2)}) %collective-permute-start.22) | collective-permute-done | bytes 221216 | tf_op jit(solution)/shard_map/ppermute | solution.py:255
  173.8 3.8 %collective-permute-start.23 = (bf16[192,576]{1,0:T(8,128)(2,1)S(1)}, bf16[192,576]{1,0:T(8,128)(2,1)S(1)}, u32[]{:S(2)}, u32[]{:S(2)}) collective-permute-start(bf16[192,576]{1,0:T(8,128)(2,1)S(1)} %add_convert_fusion.1), channel_id=1, source_target_pairs={{0,7},{1,0},{2,1},{3,2},{4,3},{5,4},{6,5},{7,6},{8,15},{9,8},{10,9... | collective-permute-start | bytes 663560 | tf_op jit(solution)/shard_map/ppermute | solution.py:255
  177.6 0.6 collective-permute-done.18
  178.4 3.0 %collective-permute-done.23 = bf16[192,576]{1,0:T(8,128)(2,1)S(1)} collective-permute-done((bf16[192,576]{1,0:T(8,128)(2,1)S(1)}, bf16[192,576]{1,0:T(8,128)(2,1)S(1)}, u32[]{:S(2)}, u32[]{:S(2)}) %collective-permute-start.23) | collective-permute-done | bytes 221216 | tf_op jit(solution)/shard_map/ppermute | solution.py:255
  181.4 3.8 %collective-permute-start.24 = (bf16[192,576]{1,0:T(8,128)(2,1)S(1)}, bf16[192,576]{1,0:T(8,128)(2,1)S(1)}, u32[]{:S(2)}, u32[]{:S(2)}) collective-permute-start(bf16[192,576]{1,0:T(8,128)(2,1)S(1)} %add_convert_fusion), channel_id=1, source_target_pairs={{0,7},{1,0},{2,1},{3,2},{4,3},{5,4},{6,5},{7,6},{8,15},{9,8},{10,9... | collective-permute-start | bytes 663560 | tf_op jit(solution)/shard_map/ppermute | solution.py:255
  185.2 0.6 collective-permute-done.19
  186.0 3.0 %collective-permute-done.24.down = bf16[192,576]{1,0:T(8,128)(2,1)S(1)} collective-permute-done((bf16[192,576]{1,0:T(8,128)(2,1)S(1)}, bf16[192,576]{1,0:T(8,128)(2,1)S(1)}, u32[]{:S(2)}, u32[]{:S(2)}) %collective-permute-start.24) | collective-permute-done | bytes 221216 | tf_op jit(solution)/shard_map/ppermute | solution.py:255
  188.9 4.4 %collective-permute-done.20.up = bf16[192,576]{1,0:T(8,128)(2,1)S(1)} collective-permute-done((bf16[192,576]{1,0:T(8,128)(2,1)S(1)}, bf16[192,576]{1,0:T(8,128)(2,1)S(1)}, u32[]{:S(2)}, u32[]{:S(2)}) %collective-permute-start.20) | collective-permute-done | bytes 221216 | tf_op jit(solution)/shard_map/ppermute | solution.py:255
  193.4 0.7 copy-done.18
  194.0 2.2 %shard_map.129 = bf16[32,16,768]{2,1,0:T(8,128)(2,1)} custom-call(s32[12]{0:T(128)} %reshape.36.chosen, bf16[192,576]{1,0:T(8,128)(2,1)} %get-tuple-element.59.own, bf16[192,576]{1,0:T(8,128)(2,1)} %copy-done.18, bf16[192,576]{1,0:T(8,128)(2,1)} %copy-done.17, bf16[16,128]{1,0:T(8,128)(2,1)} %get-tuple-element.68.sums), custom_call_target="tpu_custom_call" | custom-call | flops 1000000 | bytes 2000000 | tf_op jit(solution)/shard_map/pallas_call | solution.py:558
  196.3 18.7 %all_to_all.15.got_ref = bf16[32,16,768]{2,1,0:T(8,128)(2,1)} all-to-all(bf16[32,16,768]{2,1,0:T(8,128)(2,1)} %shard_map.129), channel_id=1, replica_groups=mesh['x'=4,'y'=4,'core'=2,'tp'=8] {'x','y','core'}, dimensions={0} | all-to-all | bytes 1572864 | tf_op jit(solution)/shard_map/all_to_all | solution.py:670
  214.9 2.3 %shard_map.130 = (f32[16,16,576]{2,1,0:T(8,128)}, f32[32,2048]{1,0:T(8,128)}) custom-call(s32[32]{0:T(128)} %fusion.3.ids, bf16[32,16,768]{2,1,0:T(8,128)(2,1)} %all_to_all.15.got_ref), custom_call_target="tpu_custom_call" | custom-call | flops 1000000 | bytes 2000000 | tf_op jit(solution)/shard_map/pallas_call | solution.py:577
  (81 shorter events, 2.7 us)
Async XLA Ops:
  9.6 8.3 %collective-permute-start = (bf16[16,256,256]{2,1,0:T(8,128)(2,1)}, bf16[16,256,256]{2,1,0:T(8,128)(2,1)S(1)}, u32[]{:S(2)}, u32[]{:S(2)}) collective-permute-start(bf16[16,256,256]{2,1,0:T(8,128)(2,1)} %get-tuple-element.39.refs_0_.refs_1_.refs_2_.refs_3_), channel_id=1, source_target_pairs={{0,8},{8,0},{1,9},{9,1},{2,10},{10,2},{3,11},{11,3},{4,12},{12,4},... | collective-permute-start | bytes 6291464 | tf_op jit(solution)/shard_map/ppermute | solution.py:255
  9.7 8.1 %collective-permute-start.1 = (bf16[256,1024]{1,0:T(8,128)(2,1)}, bf16[256,1024]{1,0:T(8,128)(2,1)S(1)}, u32[]{:S(2)}, u32[]{:S(2)}) collective-permute-start(bf16[256,1024]{1,0:T(8,128)(2,1)} %get-tuple-element.41), channel_id=1, source_target_pairs={{0,8},{8,0},{1,9},{9,1},{2,10},{10,2},{3,11},{11,3},{4,12},{12,4},... | collective-permute-start | bytes 1572872 | tf_op jit(solution)/shard_map/ppermute | solution.py:255
  10.2 21.6 %all-to-all-start = ((bf16[32,16,640]{2,1,0:T(8,128)(2,1)}), bf16[32,16,640]{2,1,0:T(8,128)(2,1)S(1)}, u32[]{:S(2)}, u32[]{:S(2)}) async-start(bf16[32,16,640]{2,1,0:T(8,128)(2,1)} %get-tuple-element.38), calls=%async_computation | async-start | bytes 1310720 | tf_op jit(solution)/shard_map/all_to_all | solution.py:625
  17.8 0.8 copy-start.9
  17.8 1.5 copy-start
  31.8 1.9 copy-start.2
  36.1 19.5 %all-to-all-start.1 = ((bf16[32,16,768]{2,1,0:T(8,128)(2,1)}), bf16[32,16,768]{2,1,0:T(8,128)(2,1)S(1)}, u32[]{:S(2)}, u32[]{:S(2)}) async-start(bf16[32,16,768]{2,1,0:T(8,128)(2,1)} %shard_map.122), calls=%async_computation.1 | async-start | bytes 1572864 | tf_op jit(solution)/shard_map/all_to_all | solution.py:646
  45.0 31.9 %collective-permute-start.10 = (bf16[4,256,1024]{2,1,0:T(8,128)(2,1)}, bf16[4,256,1024]{2,1,0:T(8,128)(2,1)S(1)}, u32[]{:S(2)}, u32[]{:S(2)}) collective-permute-start(bf16[4,256,1024]{2,1,0:T(8,128)(2,1)} %get-tuple-element.47), channel_id=1, source_target_pairs={{0,192},{8,56},{16,208},{24,8},{32,224},{40,24},{48,240},{56,40},{... | collective-permute-start | bytes 6291464 | tf_op jit(solution)/shard_map/ppermute | solution.py:251
  45.2 31.7 %collective-permute-start.9 = (bf16[4,256,1024]{2,1,0:T(8,128)(2,1)}, bf16[4,256,1024]{2,1,0:T(8,128)(2,1)}, u32[]{:S(2)}, u32[]{:S(2)}) collective-permute-start(bf16[4,256,1024]{2,1,0:T(8,128)(2,1)} %get-tuple-element.46), channel_id=1, source_target_pairs={{0,64},{8,24},{16,80},{24,40},{32,96},{40,56},{48,112},{56,8},{64,... | collective-permute-start | bytes 6291464 | tf_op jit(solution)/shard_map/ppermute | solution.py:251
  55.5 0.9 copy-start.5
  58.3 12.7 %collective-permute-start.2 = (bf16[208,576]{1,0:T(8,128)(2,1)}, bf16[208,576]{1,0:T(8,128)(2,1)S(1)}, u32[]{:S(2)}, u32[]{:S(2)}) collective-permute-start(bf16[208,576]{1,0:T(8,128)(2,1)} %get-tuple-element.44.refs_0_), channel_id=1, source_target_pairs={{0,7},{1,0},{2,1},{3,2},{4,3},{5,4},{6,5},{7,6},{8,15},{9,8},{10,9... | collective-permute-start | bytes 718856 | tf_op jit(solution)/shard_map/ppermute | solution.py:255
  71.0 5.9 %copy-start.12 = (bf16[208,576]{1,0:T(8,128)(2,1)}, bf16[208,576]{1,0:T(8,128)(2,1)S(1)}, u32[]{:S(2)}) copy-start(bf16[208,576]{1,0:T(8,128)(2,1)S(1)} %collective-permute-done.2.mark.refs_1_) | copy-start | bytes 718852
  76.9 1.3 copy-start.1
  78.2 6.4 %copy-start.19 = (bf16[208,576]{1,0:T(8,128)(2,1)S(1)}, bf16[208,576]{1,0:T(8,128)(2,1)}, u32[]{:S(2)}) copy-start(bf16[208,576]{1,0:T(8,128)(2,1)} %get-tuple-element.44.refs_0_) | copy-start | bytes 718852
  82.6 24.7 %collective-permute-start.11 = (bf16[2,256,1024]{2,1,0:T(8,128)(2,1)}, bf16[2,256,1024]{2,1,0:T(8,128)(2,1)S(1)}, u32[]{:S(2)}, u32[]{:S(2)}) collective-permute-start(bf16[2,256,1024]{2,1,0:T(8,128)(2,1)} %get-tuple-element.50), channel_id=1, source_target_pairs={{0,64},{8,24},{16,80},{24,40},{32,96},{40,56},{48,112},{56,8},{64,... | collective-permute-start | bytes 3145736 | tf_op jit(solution)/shard_map/ppermute | solution.py:251
  83.8 23.5 %collective-permute-start.12 = (bf16[2,256,1024]{2,1,0:T(8,128)(2,1)}, bf16[2,256,1024]{2,1,0:T(8,128)(2,1)S(1)}, u32[]{:S(2)}, u32[]{:S(2)}) collective-permute-start(bf16[2,256,1024]{2,1,0:T(8,128)(2,1)} %get-tuple-element.51), channel_id=1, source_target_pairs={{0,192},{8,56},{16,208},{24,8},{32,224},{40,24},{48,240},{56,40},{... | collective-permute-start | bytes 3145736 | tf_op jit(solution)/shard_map/ppermute | solution.py:251
  84.6 13.1 %collective-permute-start.6 = (bf16[208,576]{1,0:T(8,128)(2,1)S(1)}, bf16[208,576]{1,0:T(8,128)(2,1)S(1)}, u32[]{:S(2)}, u32[]{:S(2)}) collective-permute-start(bf16[208,576]{1,0:T(8,128)(2,1)S(1)} %copy-done.19), channel_id=1, source_target_pairs={{0,1},{1,2},{2,3},{3,4},{4,5},{5,6},{6,7},{7,0},{8,9},{9,10},{10,1... | collective-permute-start | bytes 718856 | tf_op jit(solution)/shard_map/ppermute | solution.py:255
  86.5 11.1 %collective-permute-start.3 = (bf16[208,576]{1,0:T(8,128)(2,1)}, bf16[208,576]{1,0:T(8,128)(2,1)S(1)}, u32[]{:S(2)}, u32[]{:S(2)}) collective-permute-start(bf16[208,576]{1,0:T(8,128)(2,1)} %copy-done.12), channel_id=1, source_target_pairs={{0,7},{1,0},{2,1},{3,2},{4,3},{5,4},{6,5},{7,6},{8,15},{9,8},{10,9... | collective-permute-start | bytes 718856 | tf_op jit(solution)/shard_map/ppermute | solution.py:255
  97.6 38.2 %copy-start.20 = (bf16[208,576]{1,0:T(8,128)(2,1)}, bf16[208,576]{1,0:T(8,128)(2,1)S(1)}, u32[]{:S(2)}) copy-start(bf16[208,576]{1,0:T(8,128)(2,1)S(1)} %collective-permute-done.6.refs_7_) | copy-start | bytes 718852
  97.6 9.6 %collective-permute-start.7 = (bf16[208,576]{1,0:T(8,128)(2,1)S(1)}, bf16[208,576]{1,0:T(8,128)(2,1)S(1)}, u32[]{:S(2)}, u32[]{:S(2)}) collective-permute-start(bf16[208,576]{1,0:T(8,128)(2,1)S(1)} %collective-permute-done.6.refs_7_), channel_id=1, source_target_pairs={{0,1},{1,2},{2,3},{3,4},{4,5},{5,6},{6,7},{7,0},{8,9},{9,10},{10,1... | collective-permute-start | bytes 718856 | tf_op jit(solution)/shard_map/ppermute | solution.py:255
  97.7 38.2 %copy-start.21 = (bf16[208,576]{1,0:T(8,128)(2,1)}, bf16[208,576]{1,0:T(8,128)(2,1)S(1)}, u32[]{:S(2)}) copy-start(bf16[208,576]{1,0:T(8,128)(2,1)S(1)} %collective-permute-done.3.refs_2_) | copy-start | bytes 718852
  97.7 9.6 %collective-permute-start.4 = (bf16[208,576]{1,0:T(8,128)(2,1)S(1)}, bf16[208,576]{1,0:T(8,128)(2,1)S(1)}, u32[]{:S(2)}, u32[]{:S(2)}) collective-permute-start(bf16[208,576]{1,0:T(8,128)(2,1)S(1)} %collective-permute-done.3.refs_2_), channel_id=1, source_target_pairs={{0,7},{1,0},{2,1},{3,2},{4,3},{5,4},{6,5},{7,6},{8,15},{9,8},{10,9... | collective-permute-start | bytes 718856 | tf_op jit(solution)/shard_map/ppermute | solution.py:255
  107.3 0.7 copy-start.10
  107.3 0.9 copy-start.11
  107.3 1.2 copy-start.3
  107.3 1.5 copy-start.4
  113.5 16.3 %collective-permute-start.13 = (bf16[256,1024]{1,0:T(8,128)(2,1)}, bf16[256,1024]{1,0:T(8,128)(2,1)S(1)}, u32[]{:S(2)}, u32[]{:S(2)}) collective-permute-start(bf16[256,1024]{1,0:T(8,128)(2,1)} %get-tuple-element.53), channel_id=1, source_target_pairs={{0,16},{8,72},{16,32},{24,88},{32,48},{40,104},{48,0},{56,120},{64... | collective-permute-start | bytes 1572872 | tf_op jit(solution)/shard_map/ppermute | solution.py:251
  113.6 16.2 %collective-permute-start.14 = (bf16[256,1024]{1,0:T(8,128)(2,1)}, bf16[256,1024]{1,0:T(8,128)(2,1)S(1)}, u32[]{:S(2)}, u32[]{:S(2)}) collective-permute-start(bf16[256,1024]{1,0:T(8,128)(2,1)} %get-tuple-element.54), channel_id=1, source_target_pairs={{0,32},{8,136},{16,48},{24,152},{32,0},{40,168},{48,16},{56,184},{... | collective-permute-start | bytes 1572872 | tf_op jit(solution)/shard_map/ppermute | solution.py:251
  113.8 16.9 %collective-permute-start.15 = (bf16[256,1024]{1,0:T(8,128)(2,1)}, bf16[256,1024]{1,0:T(8,128)(2,1)S(1)}, u32[]{:S(2)}, u32[]{:S(2)}) collective-permute-start(bf16[256,1024]{1,0:T(8,128)(2,1)} %get-tuple-element.55), channel_id=1, source_target_pairs={{0,48},{8,200},{16,0},{24,216},{32,16},{40,232},{48,32},{56,248},{... | collective-permute-start | bytes 1572872 | tf_op jit(solution)/shard_map/ppermute | solution.py:251
  117.0 17.7 %collective-permute-start.8 = (bf16[208,576]{1,0:T(8,128)(2,1)}, bf16[208,576]{1,0:T(8,128)(2,1)S(1)}, u32[]{:S(2)}, u32[]{:S(2)}) collective-permute-start(bf16[208,576]{1,0:T(8,128)(2,1)} %copy-done.10), channel_id=1, source_target_pairs={{0,1},{1,2},{2,3},{3,4},{4,5},{5,6},{6,7},{7,0},{8,9},{9,10},{10,1... | collective-permute-start | bytes 718856 | tf_op jit(solution)/shard_map/ppermute | solution.py:255
  117.1 17.6 %collective-permute-start.5 = (bf16[208,576]{1,0:T(8,128)(2,1)}, bf16[208,576]{1,0:T(8,128)(2,1)S(1)}, u32[]{:S(2)}, u32[]{:S(2)}) collective-permute-start(bf16[208,576]{1,0:T(8,128)(2,1)} %copy-done.11), channel_id=1, source_target_pairs={{0,7},{1,0},{2,1},{3,2},{4,3},{5,4},{6,5},{7,6},{8,15},{9,8},{10,9... | collective-permute-start | bytes 718856 | tf_op jit(solution)/shard_map/ppermute | solution.py:255
  129.8 0.9 copy-start.6
  129.8 1.0 copy-start.7
  130.7 0.8 copy-start.8
  134.1 1.7 collective-permute-start.16
  134.7 1.1 copy-start.22
  134.8 1.1 copy-start.23
  135.8 0.7 copy-start.24
  158.1 15.7 %copy-start.16 = (bf16[192,576]{1,0:T(8,128)(2,1)S(1)}, bf16[192,576]{1,0:T(8,128)(2,1)}, u32[]{:S(2)}) copy-start(bf16[192,576]{1,0:T(8,128)(2,1)} %get-tuple-element.65) | copy-start | bytes 663556
  158.1 20.1 %copy-start.15 = (bf16[192,576]{1,0:T(8,128)(2,1)S(1)}, bf16[192,576]{1,0:T(8,128)(2,1)}, u32[]{:S(2)}) copy-start(bf16[192,576]{1,0:T(8,128)(2,1)} %get-tuple-element.61) | copy-start | bytes 663556
  158.1 23.2 %copy-start.14 = (bf16[192,576]{1,0:T(8,128)(2,1)S(1)}, bf16[192,576]{1,0:T(8,128)(2,1)}, u32[]{:S(2)}) copy-start(bf16[192,576]{1,0:T(8,128)(2,1)} %get-tuple-element.64) | copy-start | bytes 663556
  158.2 6.3 %collective-permute-start.21 = (bf16[96,576]{1,0:T(8,128)(2,1)}, bf16[96,576]{1,0:T(8,128)(2,1)S(1)}, u32[]{:S(2)}, u32[]{:S(2)}) collective-permute-start(bf16[96,576]{1,0:T(8,128)(2,1)} %get-tuple-element.67), channel_id=1, source_target_pairs={{0,7},{1,0},{2,1},{3,2},{4,3},{5,4},{6,5},{7,6},{8,15},{9,8},{10,9... | collective-permute-start | bytes 331784 | tf_op jit(solution)/shard_map/ppermute | solution.py:255
  162.2 23.6 %copy-start.13 = (bf16[192,576]{1,0:T(8,128)(2,1)S(1)}, bf16[192,576]{1,0:T(8,128)(2,1)}, u32[]{:S(2)}) copy-start(bf16[192,576]{1,0:T(8,128)(2,1)} %get-tuple-element.60) | copy-start | bytes 663556
  162.2 6.9 %collective-permute-start.17 = (bf16[96,576]{1,0:T(8,128)(2,1)}, bf16[96,576]{1,0:T(8,128)(2,1)S(1)}, u32[]{:S(2)}, u32[]{:S(2)}) collective-permute-start(bf16[96,576]{1,0:T(8,128)(2,1)} %get-tuple-element.63), channel_id=1, source_target_pairs={{0,1},{1,2},{2,3},{3,4},{4,5},{5,6},{6,7},{7,0},{8,9},{9,10},{10,1... | collective-permute-start | bytes 331784 | tf_op jit(solution)/shard_map/ppermute | solution.py:255
  165.4 8.4 %collective-permute-start.22 = (bf16[192,576]{1,0:T(8,128)(2,1)S(1)}, bf16[192,576]{1,0:T(8,128)(2,1)S(1)}, u32[]{:S(2)}, u32[]{:S(2)}) collective-permute-start(bf16[192,576]{1,0:T(8,128)(2,1)S(1)} %pad_maximum_fusion.1), channel_id=1, source_target_pairs={{0,7},{1,0},{2,1},{3,2},{4,3},{5,4},{6,5},{7,6},{8,15},{9,8},{10,9... | collective-permute-start | bytes 663560 | tf_op jit(solution)/shard_map/ppermute | solution.py:255
  170.1 8.2 %collective-permute-start.18 = (bf16[192,576]{1,0:T(8,128)(2,1)S(1)}, bf16[192,576]{1,0:T(8,128)(2,1)S(1)}, u32[]{:S(2)}, u32[]{:S(2)}) collective-permute-start(bf16[192,576]{1,0:T(8,128)(2,1)S(1)} %pad_maximum_fusion), channel_id=1, source_target_pairs={{0,1},{1,2},{2,3},{3,4},{4,5},{5,6},{6,7},{7,0},{8,9},{9,10},{10,1... | collective-permute-start | bytes 663560 | tf_op jit(solution)/shard_map/ppermute | solution.py:255
  173.8 7.5 %collective-permute-start.23 = (bf16[192,576]{1,0:T(8,128)(2,1)S(1)}, bf16[192,576]{1,0:T(8,128)(2,1)S(1)}, u32[]{:S(2)}, u32[]{:S(2)}) collective-permute-start(bf16[192,576]{1,0:T(8,128)(2,1)S(1)} %add_convert_fusion.1), channel_id=1, source_target_pairs={{0,7},{1,0},{2,1},{3,2},{4,3},{5,4},{6,5},{7,6},{8,15},{9,8},{10,9... | collective-permute-start | bytes 663560 | tf_op jit(solution)/shard_map/ppermute | solution.py:255
  178.3 7.5 %collective-permute-start.19 = (bf16[192,576]{1,0:T(8,128)(2,1)S(1)}, bf16[192,576]{1,0:T(8,128)(2,1)S(1)}, u32[]{:S(2)}, u32[]{:S(2)}) collective-permute-start(bf16[192,576]{1,0:T(8,128)(2,1)S(1)} %add_convert_fusion.3), channel_id=1, source_target_pairs={{0,1},{1,2},{2,3},{3,4},{4,5},{5,6},{6,7},{7,0},{8,9},{9,10},{10,1... | collective-permute-start | bytes 663560 | tf_op jit(solution)/shard_map/ppermute | solution.py:255
  181.4 7.5 %collective-permute-start.24 = (bf16[192,576]{1,0:T(8,128)(2,1)S(1)}, bf16[192,576]{1,0:T(8,128)(2,1)S(1)}, u32[]{:S(2)}, u32[]{:S(2)}) collective-permute-start(bf16[192,576]{1,0:T(8,128)(2,1)S(1)} %add_convert_fusion), channel_id=1, source_target_pairs={{0,7},{1,0},{2,1},{3,2},{4,3},{5,4},{6,5},{7,6},{8,15},{9,8},{10,9... | collective-permute-start | bytes 663560 | tf_op jit(solution)/shard_map/ppermute | solution.py:255
  185.9 7.5 %collective-permute-start.20 = (bf16[192,576]{1,0:T(8,128)(2,1)S(1)}, bf16[192,576]{1,0:T(8,128)(2,1)S(1)}, u32[]{:S(2)}, u32[]{:S(2)}) collective-permute-start(bf16[192,576]{1,0:T(8,128)(2,1)S(1)} %add_convert_fusion.2), channel_id=1, source_target_pairs={{0,1},{1,2},{2,3},{3,4},{4,5},{5,6},{6,7},{7,0},{8,9},{9,10},{10,1... | collective-permute-start | bytes 663560 | tf_op jit(solution)/shard_map/ppermute | solution.py:255
  188.9 4.4 %copy-start.17 = (bf16[192,576]{1,0:T(8,128)(2,1)}, bf16[192,576]{1,0:T(8,128)(2,1)S(1)}, u32[]{:S(2)}) copy-start(bf16[192,576]{1,0:T(8,128)(2,1)S(1)} %collective-permute-done.24.down) | copy-start | bytes 663556
  193.4 0.7 copy-start.18
